TPU v7x, 512 devices: a whole 4x8x8 slice. The times are simulated.
512 devices in a mesh: bunch: 8 (over x, core), dom: 64 (over z, y).
Axes of the slice: x: 4, y: 8, z: 8, core: 2. Of those that a mesh axis runs over, the one named last changes fastest.
Arguments:
- coords: bfloat16 [512, 2, 32768], P('bunch', None, 'dom'), may hold values from -6 to 6
- slice_index: int32 [512, 32768], P('bunch', 'dom'), may hold values from 0 to 511
- history: float32 [512, 16, 2, 512], P('bunch'), may hold values from -6 to 6
- turn_coef: float32 [16, 2], replicated, may hold values from 0.02 to 0.2
- fill: int32 [512], replicated, may hold values from 0 to 1023, as said below
- panels: bfloat16 [2, 4, 512, 512], P(None, None, 'dom'), may hold values from -0.25 to 0.25
Outputs:
- particle_kick: bfloat16 [512, 2, 32768], P('bunch', None, 'dom')
Inputs may be any that keep to these rules, and one draw needn't show every extreme that they name: fill rises strictly along the train; the first bunch sits in bucket 0 and the last in bucket 1024 - 1.
All inputs are finite; a program needn't handle non-finite values.
Results may differ from a plain program's by a relative error of at most 0.0049.
Values may be sent and summed in bfloat16 or wider, within the bound.
No kernel may reach another device: no remote copies, remote signals or barrier semaphores. Data moves between devices by JAX's collectives and lax.ppermute only.
A program may use at most 64 MiB of HBM per device.

v0:
```python
import math

import jax
import jax.numpy as jnp
from jax import lax
from jax.sharding import PartitionSpec as P


def shifted_2(value, axis, steps):
    count = lax.axis_size(axis)
    pairs = [(source, (source + steps) % count) for source in range(count)]
    return lax.ppermute(value, axis, pairs)


def combine(stored, current, turn_coef):
    carried = jnp.einsum("btps,tp->bps", stored, turn_coef, precision=lax.Precision.HIGHEST)
    return (current + carried).astype(jnp.bfloat16)


def local(coords, slice_index, history, turn_coef, fill, panels):
    bunches = coords.shape[0]
    count = coords.shape[2]
    slices = panels.shape[3]
    reach = panels.shape[1]
    back = reach - 1
    group = math.gcd(bunches, 8)
    scale = (slices / (count * lax.axis_size("dom"))) ** 0.5
    grouped_coords = coords.reshape(bunches // group, group, 2, count)
    grouped_index = slice_index.reshape(bunches // group, group, count)

    def partial_moment(pieces):
        block_coords, block_index = pieces
        columns = lax.broadcasted_iota(jnp.int32, (1, 1, slices), 2)
        onehot = (block_index[:, :, None] == columns).astype(jnp.bfloat16)
        return jnp.einsum("gpi,gis->gps", block_coords, onehot, preferred_element_type=jnp.float32)

    partials = lax.map(partial_moment, (grouped_coords, grouped_index)).reshape(bunches, 2, slices)
    moment = lax.psum(partials, "dom") * scale
    own_source = combine(history, moment, turn_coef)
    prev_stored, prev_moment = shifted_2(
        (history[bunches - back :], moment[bunches - back :]), "bunch", 1
    )
    prev_source = combine(prev_stored, prev_moment, turn_coef)
    extended = jnp.concatenate([prev_source, own_source], 0)
    total_bunches = bunches * lax.axis_size("bunch")
    first = lax.axis_index("bunch") * bunches
    positions = jnp.mod(first - back + jnp.arange(bunches + back, dtype=jnp.int32), total_bunches)
    ext_fill = jnp.take(fill, positions)
    cycle_size = 2 * total_bunches
    gap_rows = []
    shifted_rows = []
    for offset in range(reach):
        gap_rows.append(
            jnp.mod(ext_fill[back:] - ext_fill[back - offset : back - offset + bunches], cycle_size)
        )
        shifted_rows.append(extended[back - offset : back - offset + bunches])
    gaps = jnp.stack(gap_rows, 0)
    shifted = jnp.stack(shifted_rows, 0)
    chosen = []
    for panel in range(reach):
        hits = (gaps == panel)[:, :, None, None]
        chosen.append(jnp.sum(jnp.where(hits, shifted, jnp.zeros((), jnp.bfloat16)), axis=0))
    selected = jnp.stack(chosen, 0)
    result = jnp.einsum(
        "pksj,kbpj->bps",
        lax.all_gather(panels, "dom", axis=2, tiled=True),
        selected,
        preferred_element_type=jnp.float32,
    )
    kick = result.astype(jnp.bfloat16)
    grouped_kick = kick.reshape(bunches // group, group, 2, slices)

    def interpolate(pieces):
        block_kick, block_index = pieces
        columns = lax.broadcasted_iota(jnp.int32, (1, 1, slices), 2)
        onehot = (block_index[:, :, None] == columns).astype(jnp.bfloat16)
        picked = jnp.einsum("gps,gis->gpi", block_kick, onehot, preferred_element_type=jnp.float32)
        return picked.astype(jnp.bfloat16)

    return lax.map(interpolate, (grouped_kick, grouped_index)).reshape(bunches, 2, count)


def solution(mesh):
    return jax.shard_map(
        local,
        mesh=mesh,
        in_specs=(
            P("bunch", None, "dom"),
            P("bunch", "dom"),
            P("bunch", None, None, None),
            P(),
            P(),
            P(None, None, "dom", None),
        ),
        out_specs=P("bunch", None, "dom"),
        check_vma=False,
    )
```

profile of v0, /device:TPU:8, one launch (start us, length us, event | category | flops | bytes accessed | tf_op | source)
XLA Modules:
  0.0 318.5 jit_solution(2210444123989930070)
XLA Ops:
  6.5 0.0 copy-start
  6.5 0.0 all-reduce.2.cloned.1.call-start
  6.5 0.0 copy-start.1
  6.5 27.5 %while.20 = (s32[]{:T(128)}, f32[8,8,2,512]{3,2,1,0:T(2,128)}, bf16[8,8,2,512]{3,2,1,0:T(2,128)(2,1)}, s32[8,8,512]{2,1,0:T(8,128)}, s32[]{:T(128)}) while((s32[]{:T(128)}, f32[8,8,2,512]{3,2,1,0:T(2,128)}, bf16[8,8,2,512]{3,2,1,0:T(2,128)(2,1)}, s32[8,8,512]{2,1,0:T(8,128)}, s32[]{:T(128)}) %tuple.59), condition=%wide.region_1.2_spmd, body=%wide.region_0.1_spmd.sunk | while | flops 10485762 | bytes 99393 | solution.py:37
  6.5 0.7 dynamic-slice_bitcast_fusion.4
  7.3 2.7 fusion.53
  10.0 0.7 dynamic-slice_bitcast_fusion.4
  10.7 2.7 fusion.53
  13.5 0.7 dynamic-slice_bitcast_fusion.4
  14.2 2.7 fusion.53
  16.9 0.7 dynamic-slice_bitcast_fusion.4
  17.6 2.7 fusion.53
  20.3 0.7 dynamic-slice_bitcast_fusion.4
  21.0 2.7 fusion.53
  23.8 0.7 dynamic-slice_bitcast_fusion.4
  24.5 2.7 fusion.53
  27.2 0.7 dynamic-slice_bitcast_fusion.4
  27.9 2.7 fusion.53
  30.7 0.7 dynamic-slice_bitcast_fusion.4
  31.4 2.7 fusion.53
  34.1 0.0 all-reduce.2.cloned.1.call-update
  34.1 0.0 all-gather.2.cloned.1.call-start
  34.2 0.7 all-gather.2.cloned.1.call-update
  34.9 0.9 slice.36
  35.8 0.0 collective-permute-start.1
  35.9 0.0 copy-done
  35.9 1.3 gather_fusion
  37.2 0.1 fusion.36
  37.3 0.1 broadcast_compare_fusion.2
  37.4 0.0 copy-done.1
  37.4 4.7 %fusion.12 = f32[2,1,64,512]{3,1,2,0:T(1,128)S(1)} fusion(f32[16,2,1,1]{0,2,3,1:T(1,128)S(1)} %bitcast.90, f32[64,16,2,512]{3,2,1,0:T(2,128)} %param.12), kind=kOutput, calls=%fused_computation.19 | convolution fusion | flops 12582912 | bytes 4456576 | tf_op jit(solution)/shard_map/btps,tp->bps/dot_general | solution.py:16
  42.1 148.2 %all-reduce.2.cloned.1.call-done = f32[64,2,512]{2,1,0:T(2,128)} async-done(((f32[64,2,512]{2,1,0:T(2,128)}), f32[64,2,512]{2,1,0:T(2,128)}) %all-reduce.2.cloned.1.call-update) | async-done | bytes 262160 | tf_op jit(solution)/shard_map/psum | solution.py:38
  190.3 1.3 broadcast_multiply_fusion
  191.6 0.0 collective-permute-start
  191.7 0.0 collective-permute-done.1
  191.7 0.2 fusion.28
  191.9 4.1 %collective-permute-done = f32[3,2,512]{2,1,0:T(2,128)S(1)} collective-permute-done((f32[3,2,512]{2,1,0:T(2,128)S(1)}, f32[3,2,512]{2,1,0:T(2,128)S(1)}, u32[]{:S(2)}, u32[]{:S(2)}) %collective-permute-start) | collective-permute-done | bytes 12320 | tf_op jit(solution)/shard_map/ppermute | solution.py:12
  196.0 0.2 fusion.33
  196.2 3.3 %fusion.16 = (bf16[64,2,512]{2,1,0:T(2,128)(2,1)S(1)}, bf16[64,2,512]{2,1,0:T(2,128)(2,1)S(1)}, bf16[64,2,512]{2,1,0:T(2,128)(2,1)S(1)}, bf16[64,2,512]{2,1,0:T(2,128)(2,1)S(1)}) fusion(pred[4,64]{1,0:T(4,128)(4,1)S(1)} %get-tuple-element.92, pred[4,64]{1,0:T(4,128)(4,1)S(1)} %get-tuple-element.91, pred[4,64]{1,0:T(4,128)(4,1)S(1)} %get-tuple-element.90, ...), kind=kLoop, calls=%fused_computation.28 | loop fusion | flops 2621440 | bytes 1049600 | tf_op jit(solution)/shard_map/reduce_sum | solution.py:62
  199.6 83.4 %all-gather.2.cloned.1.call-done = bf16[2,4,512,512]{3,2,1,0:T(8,128)(2,1)} async-done(((bf16[2,4,8,512]{3,2,1,0:T(8,128)(2,1)}), bf16[2,4,512,512]{3,2,1,0:T(8,128)(2,1)}) %all-gather.2.cloned.1.call-update) | async-done | bytes 4194320 | tf_op jit(solution)/shard_map/all_gather | solution.py:66
  283.0 3.6 %fusion.15 = bf16[8,8,2,512]{3,1,0,2:T(8,128)(2,1)S(1)} fusion(bf16[2,4,512,512]{3,2,1,0:T(8,128)(2,1)} %all-gather.2.cloned.1.call-done, bf16[1,64,2,512]{3,1,0,2:T(8,128)(2,1)S(1)} %get-tuple-element.96, bf16[1,64,2,512]{3,1,0,2:T(8,128)(2,1)S(1)} %get-tuple-element.97, bf16[1,64,2,512]{3,1,0,2:T(8,128)(2,1)S(1)} %get-tuple-element.98, ...), kind=kOutput, calls=%fused_computation.23 | convolution fusion | flops 269287424 | bytes 4849664 | tf_op jit(solution)/shard_map/pksj,kbpj->bps/dot_general | solution.py:64
  286.6 25.0 %while.21 = (s32[]{:T(128)}, bf16[8,8,2,512]{3,2,1,0:T(2,128)(2,1)}, bf16[8,8,2,512]{3,1,0,2:T(8,128)(2,1)S(1)}, s32[8,8,512]{2,1,0:T(8,128)}, s32[]{:T(128)}) while((s32[]{:T(128)}, bf16[8,8,2,512]{3,2,1,0:T(2,128)(2,1)}, bf16[8,8,2,512]{3,1,0,2:T(8,128)(2,1)S(1)}, s32[8,8,512]{2,1,0:T(8,128)}, s32[]{:T(128)}) %tuple.58), condition=%wide.region_8.9_spmd, body=%wide.region_7.8_spmd.sunk | while | flops 10493954 | bytes 115269 | solution.py:80
  286.6 0.7 dynamic-slice_bitcast_fusion.5
  287.4 2.4 fusion.54
  289.8 0.7 dynamic-slice_bitcast_fusion.5
  290.5 2.4 fusion.54
  292.9 0.7 dynamic-slice_bitcast_fusion.5
  293.6 2.4 fusion.54
  296.0 0.7 dynamic-slice_bitcast_fusion.5
  296.7 2.4 fusion.54
  299.1 0.7 dynamic-slice_bitcast_fusion.5
  299.9 2.4 fusion.54
  302.3 0.7 dynamic-slice_bitcast_fusion.5
  303.0 2.4 fusion.54
  305.4 0.7 dynamic-slice_bitcast_fusion.5
  306.1 2.4 fusion.54
  308.5 0.7 dynamic-slice_bitcast_fusion.5
  309.2 2.4 fusion.54
  (19 shorter events, 0.1 us)
Async XLA Ops:
  6.5 29.4 %copy-start = (s32[512]{0:T(512)S(1)}, s32[512]{0:T(512)}, u32[]{:S(2)}) copy-start(s32[512]{0:T(512)} %param.14) | copy-start | bytes 6148
  6.5 183.8 %all-reduce.2.cloned.1.call-start = ((), (), s32[]{:S(2)}) async-start(), calls=%async_computation | async-start | bytes 524288 | tf_op jit(solution)/shard_map/psum | solution.py:38
  6.5 30.8 %copy-start.1 = (f32[16,2]{0,1:T(2,128)S(1)}, f32[16,2]{0,1:T(2,128)}, u32[]{:S(2)}) copy-start(f32[16,2]{0,1:T(2,128)} %param.13) | copy-start | bytes 388
  34.1 248.9 %all-gather.2.cloned.1.call-start = ((), (), s32[]{:S(2)}) async-start(), calls=%async_computation.1 | async-start | bytes 4259840 | tf_op jit(solution)/shard_map/all_gather | solution.py:66
  35.8 155.8 %collective-permute-start.1 = (f32[3,16,2,512]{3,2,1,0:T(2,128)S(1)}, f32[3,16,2,512]{3,2,1,0:T(2,128)S(1)}, u32[]{:S(2)}, u32[]{:S(2)}) collective-permute-start(f32[3,16,2,512]{3,2,1,0:T(2,128)S(1)} %slice.36), channel_id=1, source_target_pairs={{0,64},{64,128},{128,192},{192,256},{256,320},{320,384},{384,448},... | collective-permute-start | bytes 589832 | tf_op jit(solution)/shard_map/ppermute | solution.py:12
  191.6 4.3 %collective-permute-start = (f32[3,2,512]{2,1,0:T(2,128)S(1)}, f32[3,2,512]{2,1,0:T(2,128)S(1)}, u32[]{:S(2)}, u32[]{:S(2)}) collective-permute-start(f32[3,2,512]{2,1,0:T(2,128)S(1)} %slice.42), channel_id=1, source_target_pairs={{0,64},{64,128},{128,192},{192,256},{256,320},{320,384},{384,448},... | collective-permute-start | bytes 36872 | tf_op jit(solution)/shard_map/ppermute | solution.py:12
Sparse Core Ops, SparseCore 0:
  34.2 156.0 all-reduce.1
  193.7 89.2 all-gather.1
where the time goes:
time: 321 us; the launch traced here: 318 us
  waiting for transfers between devices  236 us (74%)
  matrix products  49.5 us (15%)
  local copies, waits for them, and re-layouts  13.8 us (4%)
  between operations  13.6 us (4%)
  other arithmetic  5.06 us (2%)
    psum x1, waiting for transfers between devices, local(): moment = lax.psum(partials, 'dom') * scale  148 us
    all_gather x1, waiting for transfers between devices, local(): lax.all_gather(panels, 'dom', axis=2, tiled=True)  83.4 us
    dot_general x8, matrix products, partial_moment(): jnp.einsum('gpi,gis->gps', block_coords, onehot, preferred_element_type=j...  21.8 us
    dot_general x8, matrix products, interpolate(): jnp.einsum('gps,gis->gpi', block_kick, onehot, preferred_element_type=jnp...  19.2 us
  transfers between devices with their start and end apart: 4, of which 3 were waited for; matrix products, arithmetic and copies ran while one was open for 4% of the time, Pallas kernels for 0%

commit v1 on v0

v1 whole, which is shorter than its diff:
```python
import functools

import jax
import jax.numpy as jnp
from jax import lax
from jax.experimental import pallas as pl
from jax.experimental.pallas import tpu as pltpu
from jax.sharding import Mesh
from jax.sharding import PartitionSpec as P

F32 = jnp.float32
BF16 = jnp.bfloat16
LANES = 128
DOM = ("zq", "z0", "y")
ROW16 = ("z0", "y")
COL4 = ("zq",)
COL8 = ("zq", "z0")
VMEM = pl.BlockSpec(memory_space=pltpu.VMEM)
HBM = pl.BlockSpec(memory_space=pl.ANY)
PARAMS = pltpu.CompilerParams(vmem_limit_bytes=32 * 1024 * 1024)


def bunch_moment(coords_ref, index_ref, b):
    count = index_ref.shape[1]
    row = index_ref[pl.ds(b, 1), :]
    low = jnp.broadcast_to(row & (LANES - 1), (LANES, count))
    high = jnp.broadcast_to(row >> 7, (8, count))
    onehot = jnp.where(
        low == lax.broadcasted_iota(jnp.int32, (LANES, count), 0), 1.0, 0.0
    ).astype(BF16)
    planes = coords_ref[b].astype(F32)
    sub = lax.broadcasted_iota(jnp.int32, (8, count), 0)
    both = jnp.where(sub < 4, planes[0:1], planes[1:2])
    left = jnp.where(high == (sub & 3), both, 0.0).astype(BF16)
    return lax.dot_general(
        left, onehot, (((1,), (1,)), ((), ())), preferred_element_type=F32
    )


def halo_kernel(scale, coords_ref, index_ref, hist_ref, coef_ref, halo_ref, carried_ref, hist, rows, sem):
    dom = lax.axis_index(DOM)
    bunches = index_ref.shape[0]
    copy = pltpu.make_async_copy(hist_ref.at[dom], hist, sem)
    copy.start()
    for b in range(8):
        rows[pl.ds(8 * b, 8), :] = scale * bunch_moment(coords_ref, index_ref, bunches - 8 + b)
    copy.wait()
    total = jnp.zeros(hist.shape[1:], F32)
    for turn in range(hist.shape[0]):
        for_turn = jnp.concatenate(
            [jnp.full((1, 1), coef_ref[turn, 0]), jnp.full((1, 1), coef_ref[turn, 1])], 0
        )
        total = total + hist[turn] * for_turn
    for plane in range(2):
        for high in range(4):
            carried_ref[pl.ds(plane * 4 + high, 1), :] = total[
                plane : plane + 1, high * LANES : (high + 1) * LANES
            ]

    @pl.when(dom >= bunches - 8)
    def _():
        at = pl.ds(pl.multiple_of((dom - (bunches - 8)) * 8, 8), 8)
        rows[at, :] = rows[at, :] + carried_ref[...]

    for ph in range(8):
        halo_ref[ph] = rows[pl.ds(ph, 8, stride=8), :]


def moment_kernel(scale, coords_ref, index_ref, carried_ref, out_ref, rows):
    dom = lax.axis_index(DOM)
    bunches = index_ref.shape[0]

    def one(b, _):
        rows[pl.ds(pl.multiple_of(8 * b, 8), 8), :] = scale * bunch_moment(coords_ref, index_ref, b)
        return 0

    lax.fori_loop(0, bunches, one, 0, unroll=8)
    at = pl.ds(pl.multiple_of(dom * 8, 8), 8)
    rows[at, :] = rows[at, :] + carried_ref[...]
    for ph in range(8):
        for half in range(2):
            for tile in range(4):
                first = (half * 32 + tile * 8) * 8
                out_ref[ph * 2 + half, pl.ds(8 + tile * 8, 8), :] = rows[pl.ds(first + ph, 8, stride=8), :]
            if half == 1:
                out_ref[ph * 2 + half, pl.ds(0, 8), :] = jnp.zeros((8, LANES), F32)


def sum_kernel(in_ref, out_ref):
    total = in_ref[0]
    for part in range(1, in_ref.shape[0]):
        total = total + in_ref[part]
    for copy in range(out_ref.shape[0]):
        out_ref[copy] = total


def source_kernel(in_ref, out_ref):
    total = in_ref[0]
    for part in range(1, in_ref.shape[0]):
        total = total + in_ref[part]
    total = jnp.concatenate([total, jnp.zeros((8, LANES), F32)], 0).astype(BF16)
    for copy in range(out_ref.shape[0]):
        out_ref[copy] = total


def kick_kernel(total_bunches, in_ref, panels_ref, fill_ref, out_ref, source, bucket):
    bunches = 64
    first = lax.axis_index("bunch") * bunches
    sub = lax.broadcasted_iota(jnp.int32, (8, LANES), 0)
    for tile in range(9):
        column = jnp.zeros((8, LANES), jnp.int32)
        for row in range(8):
            place = first - 8 + tile * 8 + row + total_bunches
            place = jnp.where(place >= total_bunches, place - total_bunches, place)
            column = jnp.where(sub == row, fill_ref[place], column)
        bucket[pl.ds(tile * 8, 8), :] = column
    for ph in range(8):
        source[ph, pl.ds(0, 40), :] = in_ref[2 * ph].astype(F32)[0:40]
        source[ph, pl.ds(40, 32), :] = in_ref[2 * ph + 1].astype(F32)[8:40]
    cycle = 2 * total_bunches
    here = bucket[pl.ds(8, bunches), :]
    gaps = [None] + [(here - bucket[pl.ds(8 - d, bunches), :]) & (cycle - 1) for d in (1, 2, 3)]
    outs = []
    for plane in range(2):
        picked = [[], [], [], []]
        for high in range(4):
            ph = plane * 4 + high
            past = [source[ph, pl.ds(8 - d, bunches), :] for d in range(4)]
            picked[0].append(past[0].astype(BF16))
            for k in (1, 2, 3):
                value = jnp.zeros((bunches, LANES), F32)
                for d in range(1, k + 1):
                    value = jnp.where(gaps[d] == k, past[d], value)
                picked[k].append(value.astype(BF16))
        total = None
        for k in range(4):
            right = jnp.concatenate(picked[k], 1)
            left = jnp.concatenate([panels_ref[y, plane, k] for y in range(8)], 0).astype(BF16)
            part = lax.dot_general(left, right, (((1,), (1,)), ((), ())), preferred_element_type=F32)
            total = part if total is None else total + part
        outs.append(total)
    kick = jnp.concatenate(outs, 1).astype(BF16)
    for copy in range(out_ref.shape[0]):
        out_ref[copy] = kick


def lookup_kernel(kick_ref, index_ref, out_ref, table):
    bunches = index_ref.shape[0]
    for high in range(4):
        rows = jnp.concatenate([kick_ref[2 * high].astype(F32), kick_ref[2 * high + 1].astype(F32)], 0)
        table[high] = rows.T
    for block in range(bunches // 8):
        for tile in range(index_ref.shape[1] // LANES):
            index = index_ref[pl.ds(block * 8, 8), pl.ds(tile * LANES, LANES)]
            low = index & (LANES - 1)
            top = index >> 7
            found = []
            for plane in range(2):
                value = None
                for high in range(4):
                    row = table[high, pl.ds(plane * bunches + block * 8, 8), :]
                    got = jnp.take_along_axis(row, low, axis=1)
                    value = got if value is None else jnp.where(top == high, got, value)
                found.append(value)
            out_ref[pl.ds(block * 8, 8), :, pl.ds(tile * LANES, LANES)] = jnp.stack(found, 1).astype(BF16)


def call(kernel, out_shape, in_specs, scratch=(), out_specs=None):
    return pl.pallas_call(
        kernel,
        out_shape=out_shape,
        in_specs=in_specs,
        out_specs=VMEM if out_specs is None else out_specs,
        scratch_shapes=list(scratch),
        compiler_params=PARAMS,
    )


def exchange(value, axes):
    return lax.all_to_all(value, axes, 0, 0, tiled=True)


def local(coords, slice_index, history, turn_coef, fill, panels):
    bunches, _, count = coords.shape
    slices = panels.shape[3]
    turns = history.shape[1]
    scale = (slices / (count * lax.axis_size(DOM))) ** 0.5
    shape = jax.ShapeDtypeStruct
    smem = pl.BlockSpec(memory_space=pltpu.SMEM)

    gathered = lax.all_gather(panels.astype(F32), "y", axis=0, tiled=False)

    halo, carried = call(
        functools.partial(halo_kernel, scale),
        (shape((8, 8, LANES), F32), shape((8, LANES), F32)),
        [VMEM, VMEM, HBM, smem],
        [pltpu.VMEM((turns, 2, slices), F32), pltpu.VMEM((64, LANES), F32), pltpu.SemaphoreType.DMA],
        (VMEM, VMEM),
    )(coords, slice_index, history, turn_coef)
    ring = lax.axis_size("bunch")
    halo = lax.ppermute(halo, "bunch", [(i, (i + 1) % ring) for i in range(ring)])
    partial = call(
        functools.partial(moment_kernel, scale),
        shape((16, 40, LANES), F32),
        [VMEM, VMEM, VMEM],
        [pltpu.VMEM((bunches * 8, LANES), F32)],
    )(coords, slice_index, carried)
    partial = partial.reshape(8, 2, 40, LANES).at[:, 0, 0:8].set(halo).reshape(16, 40, LANES)
    part = exchange(partial, ROW16)
    part = call(sum_kernel, shape((4, 40, LANES), F32), [VMEM])(part)
    part = exchange(part, COL4)
    source = call(source_kernel, shape((16, 48, LANES), BF16), [VMEM])(part)
    source = exchange(source, ROW16)
    kick = call(
        functools.partial(kick_kernel, bunches * ring),
        shape((8, 64, LANES), BF16),
        [VMEM, VMEM, smem],
        [pltpu.VMEM((8, 72, LANES), F32), pltpu.VMEM((72, LANES), jnp.int32)],
    )(source, gathered, fill)
    kick = exchange(kick, COL8)
    return call(
        lookup_kernel,
        shape((bunches, 2, count), BF16),
        [VMEM, VMEM],
        [pltpu.VMEM((4, LANES, LANES), F32)],
    )(kick, slice_index)


def solution(mesh):
    fine = Mesh(mesh.devices.reshape(8, 4, 2, 8), ("bunch", "zq", "z0", "y"))
    return jax.shard_map(
        local,
        mesh=fine,
        in_specs=(
            P("bunch", None, DOM),
            P("bunch", DOM),
            P("bunch", None, None, None),
            P(),
            P(),
            P(None, None, DOM, None),
        ),
        out_specs=P("bunch", None, DOM),
        check_vma=False,
    )
```

time: 321 us -> 95.2 us (0.30)
  waiting for transfers between devices: 236 us -> 1.33 us
  blocking collectives: 0 us -> 65.8 us
  matrix products: 49.5 us -> 0 us
  local copies, waits for them, and re-layouts: 13.8 us -> 5.99 us
  Pallas kernels: 0 us -> 6.71 us
  other arithmetic: 5.06 us -> 1.51 us
    psum x1 -> x0, waiting for transfers between devices: 148 us -> none  [local(): moment = lax.psum(partials, 'dom') * scale]
    all_gather x1, waiting for transfers between devices: 83.4 us -> 0.01 us  [local(): gathered = lax.all_gather(panels.astype(F32), 'y', axis=0, tiled=False)]
    all_to_all x0 -> x4, blocking collectives: none -> 65.8 us  [exchange(): return lax.all_to_all(value, axes, 0, 0, tiled=True)]
    dot_general x19 -> x0, matrix products: 49.5 us -> none  [the longest x8 21.8 us: partial_moment(): jnp.einsum('gpi,gis->gps', block_coords, onehot, preferred_element_type=j...]
    eq x16 -> x0, local copies, waits for them, and re-layouts: 11.5 us -> none  [the longest x8 5.77 us: partial_moment(): onehot = (block_index[:, :, None] == columns).astype(jnp.bfloat16)]
    pallas_call x0 -> x6, Pallas kernels: none -> 6.71 us  [the longest x1 3.22 us: local(): call(functools.partial(moment_kernel, scale), shape((16, 40, LANES), F32)...]
    unnamed x4 -> x13, local copies, waits for them, and re-layouts: 0.01 us -> 5.99 us
    reduce_sum x1 -> x0, other arithmetic: 3.32 us -> none  [local(): jnp.sum(jnp.where(hits, shifted, jnp.zeros((), jnp.bfloat16)), axis=0)]
  transfers between devices with their start and end apart: 4 -> 2, of which waited for: 3 -> 1; matrix products, arithmetic and copies ran while one was open for 4% -> 1% of each run, Pallas kernels for 0% -> 5%
where the time goes in v1:
time: 95.2 us; the launch traced here: 94.8 us
  blocking collectives  65.8 us (69%)
  between operations  13.4 us (14%)
  Pallas kernels  6.71 us (7%)
  local copies, waits for them, and re-layouts  5.99 us (6%)
  other arithmetic  1.51 us (2%)
  waiting for transfers between devices  1.33 us (1%)
    all_to_all x4, blocking collectives, exchange(): return lax.all_to_all(value, axes, 0, 0, tiled=True)  65.8 us
    unnamed x13, local copies, waits for them, and re-layouts  5.99 us
    pallas_call x1, Pallas kernels, local(): call(functools.partial(moment_kernel, scale), shape((16, 40, LANES), F32)...  3.22 us
  transfers between devices with their start and end apart: 2, of which 1 were waited for; matrix products, arithmetic and copies ran while one was open for 1% of the time, Pallas kernels for 5%

profile of v1, /device:TPU:8, one launch (start us, length us, event | category | flops | bytes accessed | tf_op | source)
XLA Modules:
  0.0 94.8 jit_solution(17585521031689290141)
XLA Ops:
  6.5 0.0 copy-start.5
  6.5 0.0 all-gather.3.cloned.1.call-start
  6.5 1.5 %all_gather.12 = f32[2,4,8,512]{3,2,1,0:T(8,128)} convert(bf16[2,4,8,512]{3,2,1,0:T(8,128)(2,1)} %param.13) | non-fusion elementwise | flops 32768 | bytes 196608 | tf_op jit(solution)/shard_map/all_gather | solution.py:191
  8.1 0.0 all-gather.3.cloned.1.call-update
  8.1 0.8 copy.9.coef_ref
  8.8 0.0 copy-start
  8.8 2.2 %copy-done = f32[64,16,2,512]{3,2,1,0:T(2,128)S(1)} copy-done((f32[64,16,2,512]{3,2,1,0:T(2,128)S(1)}, f32[64,16,2,512]{3,2,1,0:T(2,128)}, u32[]{:S(2)}) %copy-start) | copy-done | bytes 4194328
  11.0 0.0 copy-start.1
  11.0 0.9 copy-done.1
  11.9 0.0 copy-start.4
  11.9 0.9 copy-done.4
  12.8 0.0 copy-start.2
  12.8 1.3 %shard_map.64 = (f32[8,8,128]{2,1,0:T(8,128)S(1)}, f32[8,128]{1,0:T(8,128)S(1)}) custom-call(bf16[64,2,512]{2,1,0:T(2,128)(2,1)S(1)} %copy-done.4, s32[64,512]{1,0:T(8,128)S(1)} %copy-done.1, f32[64,16,2,512]{3,2,1,0:T(2,128)S(1)} %copy-done, f32[16,2]{1,0:T(8,128)S(1)} %copy.9.coef_ref), custom_call_target="tpu_custom_call" | custom-call | tf_op jit(solution)/shard_map/pallas_call | solution.py:193
  14.1 0.0 collective-permute-start
  14.1 3.2 %shard_map.65 = f32[16,40,128]{2,1,0:T(8,128)S(1)} custom-call(bf16[64,2,512]{2,1,0:T(2,128)(2,1)S(1)} %copy-done.4, s32[64,512]{1,0:T(8,128)S(1)} %copy-done.1, f32[8,128]{1,0:T(8,128)S(1)} %get-tuple-element.19.carried_ref), custom_call_target="tpu_custom_call" | custom-call | tf_op jit(solution)/shard_map/pallas_call | solution.py:202
  17.4 1.3 %collective-permute-done = f32[8,8,128]{2,1,0:T(8,128)S(1)} collective-permute-done((f32[8,8,128]{2,1,0:T(8,128)S(1)}, f32[8,8,128]{2,1,0:T(8,128)S(1)}, u32[]{:S(2)}, u32[]{:S(2)}) %collective-permute-start) | collective-permute-done | bytes 32800 | tf_op jit(solution)/shard_map/ppermute | solution.py:201
  18.7 23.1 %all_to_all.20.in_ref = f32[16,40,128]{2,1,0:T(8,128)S(1)} all-to-all(f32[16,40,128]{2,1,0:T(8,128)S(1)} %bitcast.8), channel_id=1, replica_groups=mesh['bunch'=8,'zq'=4,'z0'=2,'y'=8] {'z0','y'}, dimensions={0} | all-to-all | bytes 655360 | tf_op jit(solution)/shard_map/all_to_all | solution.py:180
  41.8 17.7 %all_to_all.21.in_ref = f32[4,40,128]{2,1,0:T(8,128)S(1)} all-to-all(f32[4,40,128]{2,1,0:T(8,128)S(1)} %shard_map.66), channel_id=1, replica_groups=mesh['bunch'=8,'zq'=4,'z0'=2,'y'=8] {'zq'}, dimensions={0} | all-to-all | bytes 163840 | tf_op jit(solution)/shard_map/all_to_all | solution.py:180
  59.6 13.5 %all_to_all.22.in_ref = bf16[16,48,128]{2,1,0:T(8,128)(2,1)S(1)} all-to-all(bf16[16,48,128]{2,1,0:T(8,128)(2,1)S(1)} %shard_map.67), channel_id=1, replica_groups=mesh['bunch'=8,'zq'=4,'z0'=2,'y'=8] {'z0','y'}, dimensions={0} | all-to-all | bytes 393216 | tf_op jit(solution)/shard_map/all_to_all | solution.py:180
  73.1 0.0 all-gather.3.cloned.1.call-done
  73.1 0.0 copy-done.5
  73.1 0.0 copy-start.3
  73.1 1.2 %copy-done.3 = f32[16,4,8,512]{3,2,1,0:T(8,128)S(1)} copy-done((f32[16,4,8,512]{3,2,1,0:T(8,128)S(1)}, f32[16,4,8,512]{3,2,1,0:T(8,128)}, u32[]{:S(2)}) %copy-start.3) | copy-done | bytes 1048600
  74.3 1.1 %shard_map.68 = bf16[8,64,128]{2,1,0:T(8,128)(2,1)S(1)} custom-call(bf16[16,48,128]{2,1,0:T(8,128)(2,1)S(1)} %all_to_all.22.in_ref, f32[8,2,4,8,512]{4,3,2,1,0:T(8,128)S(1)} %bitcast.9, s32[512]{0:T(512)S(1)} %copy-done.5), custom_call_target="tpu_custom_call" | custom-call | tf_op jit(solution)/shard_map/pallas_call | solution.py:214
  75.4 11.5 %all_to_all.23.kick_ref = bf16[8,64,128]{2,1,0:T(8,128)(2,1)S(1)} all-to-all(bf16[8,64,128]{2,1,0:T(8,128)(2,1)S(1)} %shard_map.68), channel_id=1, replica_groups=mesh['bunch'=8,'zq'=4,'z0'=2,'y'=8] {'zq','z0'}, dimensions={0} | all-to-all | bytes 262144 | tf_op jit(solution)/shard_map/all_to_all | solution.py:180
  86.9 0.0 copy-done.2
  86.9 1.1 %shard_map.69 = bf16[64,2,512]{2,1,0:T(2,128)(2,1)} custom-call(bf16[8,64,128]{2,1,0:T(8,128)(2,1)S(1)} %all_to_all.23.kick_ref, s32[64,512]{1,0:T(8,128)S(1)} %copy-done.2), custom_call_target="tpu_custom_call" | custom-call | tf_op jit(solution)/shard_map/pallas_call | solution.py:221
  (3 shorter events, 0.0 us)
Async XLA Ops:
  6.5 66.6 %copy-start.5 = (s32[512]{0:T(512)S(1)}, s32[512]{0:T(512)}, u32[]{:S(2)}) copy-start(s32[512]{0:T(512)} %fill_ref.1) | copy-start | bytes 6148
  6.5 66.6 %all-gather.3.cloned.1.call-start = ((), (), s32[]{:S(2)}) async-start(), calls=%async_computation.4 | async-start | bytes 1179648 | tf_op jit(solution)/shard_map/all_gather | solution.py:191
  8.8 2.2 %copy-start = (f32[64,16,2,512]{3,2,1,0:T(2,128)S(1)}, f32[64,16,2,512]{3,2,1,0:T(2,128)}, u32[]{:S(2)}) copy-start(f32[64,16,2,512]{3,2,1,0:T(2,128)} %hist_ref.1) | copy-start | bytes 12582916
  11.0 0.9 copy-start.1
  11.9 0.9 copy-start.4
  12.8 74.0 %copy-start.2 = (s32[64,512]{1,0:T(8,128)S(1)}, s32[64,512]{1,0:T(8,128)}, u32[]{:S(2)}) copy-start(s32[64,512]{1,0:T(8,128)} %index_ref.5) | copy-start | bytes 393220
  14.1 4.6 %collective-permute-start = (f32[8,8,128]{2,1,0:T(8,128)S(1)}, f32[8,8,128]{2,1,0:T(8,128)S(1)}, u32[]{:S(2)}, u32[]{:S(2)}) collective-permute-start(f32[8,8,128]{2,1,0:T(8,128)S(1)} %get-tuple-element.20), channel_id=1, source_target_pairs={{0,64},{64,128},{128,192},{192,256},{256,320},{320,384},{384,448},... | collective-permute-start | bytes 98312 | tf_op jit(solution)/shard_map/ppermute | solution.py:201
  73.1 1.2 %copy-start.3 = (f32[16,4,8,512]{3,2,1,0:T(8,128)S(1)}, f32[16,4,8,512]{3,2,1,0:T(8,128)}, u32[]{:S(2)}) copy-start(f32[16,4,8,512]{3,2,1,0:T(8,128)} %all-gather.3.cloned.1.call-done) | copy-start | bytes 3145732
Sparse Core Ops, SparseCore 0:
  9.4 47.9 all-gather.2

commit v2 on v1

--- a/solution.py
+++ b/solution.py
@@ -14,9 +14,9 @@
 DOM = ("zq", "z0", "y")
 ROW16 = ("z0", "y")
 COL4 = ("zq",)
-COL8 = ("zq", "z0")
 VMEM = pl.BlockSpec(memory_space=pltpu.VMEM)
-HBM = pl.BlockSpec(memory_space=pl.ANY)
+HBM = pl.BlockSpec(memory_space=pltpu.HBM)
+WIDE = pltpu.CompilerParams(vmem_limit_bytes=60 * 1024 * 1024)
 PARAMS = pltpu.CompilerParams(vmem_limit_bytes=32 * 1024 * 1024)
 
 
@@ -37,18 +37,28 @@
     )
 
 
-def halo_kernel(scale, coords_ref, index_ref, hist_ref, coef_ref, halo_ref, carried_ref, hist, rows, sem):
+def halo_kernel(
+    scale, coords_hbm, index_hbm, hist_hbm, coef_ref, halo_ref, carried_ref, coords, index, hist, rows, sems
+):
     dom = lax.axis_index(DOM)
-    bunches = index_ref.shape[0]
-    copy = pltpu.make_async_copy(hist_ref.at[dom], hist, sem)
-    copy.start()
+    bunches = index_hbm.shape[0]
+    last = pl.ds(bunches - 8, 8)
+    copies = [
+        pltpu.make_async_copy(index_hbm.at[last], index, sems.at[0]),
+        pltpu.make_async_copy(coords_hbm.at[last], coords, sems.at[1]),
+        pltpu.make_async_copy(hist_hbm.at[dom], hist, sems.at[2]),
+    ]
+    for copy in copies:
+        copy.start()
+    copies[0].wait()
+    copies[1].wait()
     for b in range(8):
-        rows[pl.ds(8 * b, 8), :] = scale * bunch_moment(coords_ref, index_ref, bunches - 8 + b)
-    copy.wait()
+        rows[pl.ds(8 * b, 8), :] = scale * bunch_moment(coords, index, b)
+    copies[2].wait()
     total = jnp.zeros(hist.shape[1:], F32)
     for turn in range(hist.shape[0]):
         for_turn = jnp.concatenate(
-            [jnp.full((1, 1), coef_ref[turn, 0]), jnp.full((1, 1), coef_ref[turn, 1])], 0
+            [jnp.full((1, 1), coef_ref[0, turn]), jnp.full((1, 1), coef_ref[1, turn])], 0
         )
         total = total + hist[turn] * for_turn
     for plane in range(2):
@@ -135,7 +145,7 @@
         total = None
         for k in range(4):
             right = jnp.concatenate(picked[k], 1)
-            left = jnp.concatenate([panels_ref[y, plane, k] for y in range(8)], 0).astype(BF16)
+            left = panels_ref[plane, k]
             part = lax.dot_general(left, right, (((1,), (1,)), ((), ())), preferred_element_type=F32)
             total = part if total is None else total + part
         outs.append(total)
@@ -147,7 +157,7 @@
 def lookup_kernel(kick_ref, index_ref, out_ref, table):
     bunches = index_ref.shape[0]
     for high in range(4):
-        rows = jnp.concatenate([kick_ref[2 * high].astype(F32), kick_ref[2 * high + 1].astype(F32)], 0)
+        rows = jnp.concatenate([kick_ref[16 * high + part].astype(F32) for part in range(16)], 0)
         table[high] = rows.T
     for block in range(bunches // 8):
         for tile in range(index_ref.shape[1] // LANES):
@@ -165,14 +175,14 @@
             out_ref[pl.ds(block * 8, 8), :, pl.ds(tile * LANES, LANES)] = jnp.stack(found, 1).astype(BF16)
 
 
-def call(kernel, out_shape, in_specs, scratch=(), out_specs=None):
+def call(kernel, out_shape, in_specs, scratch=(), out_specs=None, params=PARAMS):
     return pl.pallas_call(
         kernel,
         out_shape=out_shape,
         in_specs=in_specs,
         out_specs=VMEM if out_specs is None else out_specs,
         scratch_shapes=list(scratch),
-        compiler_params=PARAMS,
+        compiler_params=params,
     )
 
 
@@ -188,15 +198,20 @@
     shape = jax.ShapeDtypeStruct
     smem = pl.BlockSpec(memory_space=pltpu.SMEM)
 
-    gathered = lax.all_gather(panels.astype(F32), "y", axis=0, tiled=False)
-
     halo, carried = call(
         functools.partial(halo_kernel, scale),
         (shape((8, 8, LANES), F32), shape((8, LANES), F32)),
-        [VMEM, VMEM, HBM, smem],
-        [pltpu.VMEM((turns, 2, slices), F32), pltpu.VMEM((64, LANES), F32), pltpu.SemaphoreType.DMA],
+        [HBM, HBM, HBM, smem],
+        [
+            pltpu.VMEM((8, 2, count), BF16),
+            pltpu.VMEM((8, count), jnp.int32),
+            pltpu.VMEM((turns, 2, slices), F32),
+            pltpu.VMEM((64, LANES), F32),
+            pltpu.SemaphoreType.DMA((3,)),
+        ],
         (VMEM, VMEM),
-    )(coords, slice_index, history, turn_coef)
+        WIDE,
+    )(coords, slice_index, history, turn_coef.T)
     ring = lax.axis_size("bunch")
     halo = lax.ppermute(halo, "bunch", [(i, (i + 1) % ring) for i in range(ring)])
     partial = call(
@@ -213,11 +228,11 @@
     source = exchange(source, ROW16)
     kick = call(
         functools.partial(kick_kernel, bunches * ring),
-        shape((8, 64, LANES), BF16),
+        shape((64, 8, LANES), BF16),
         [VMEM, VMEM, smem],
         [pltpu.VMEM((8, 72, LANES), F32), pltpu.VMEM((72, LANES), jnp.int32)],
-    )(source, gathered, fill)
-    kick = exchange(kick, COL8)
+    )(source, panels, fill)
+    kick = exchange(kick, DOM)
     return call(
         lookup_kernel,
         shape((bunches, 2, count), BF16),

time: 95.2 us -> 78.9 us (0.83)
  the two profiles are of different devices: /device:TPU:8 before, /device:TPU:4 now
where the time goes in v2:
time: 78.9 us; the launch traced here: 78.5 us
  blocking collectives  69.7 us (88%)
  Pallas kernels  8.07 us (10%)
    all_to_all x4, blocking collectives, exchange(): return lax.all_to_all(value, axes, 0, 0, tiled=True)  69.7 us
    pallas_call x1, Pallas kernels, local(): call(functools.partial(moment_kernel, scale), shape((16, 40, LANES), F32)...  3.2 us
    pallas_call x1, Pallas kernels, local(): call(functools.partial(halo_kernel, scale), (shape((8, 8, LANES), F32), s...  2.69 us
  transfers between devices with their start and end apart: 1, of which 0 were waited for; matrix products, arithmetic and copies ran while one was open for 0% of the time, Pallas kernels for 4%

profile of v2, /device:TPU:4, one launch (start us, length us, event | category | flops | bytes accessed | tf_op | source)
XLA Modules:
  0.0 78.5 jit_solution(2703550355706191749)
XLA Ops:
  0.0 0.0 copy-start
  0.0 0.0 copy-start.1
  0.0 0.0 copy-start.2
  0.0 0.0 copy-start.4
  0.0 2.7 %shard_map.64 = (f32[8,8,128]{2,1,0:T(8,128)}, f32[8,128]{1,0:T(8,128)}) custom-call(bf16[64,2,512]{2,1,0:T(2,128)(2,1)} %coords_ref.1, s32[64,512]{1,0:T(8,128)} %index_ref.3, f32[64,16,2,512]{3,2,1,0:T(2,128)} %hist_hbm.1, f32[2,16]{1,0:T(2,128)} %bitcast.9), custom_call_target="tpu_custom_call" | custom-call | tf_op jit(solution)/shard_map/pallas_call | solution.py:201
  2.7 0.0 collective-permute-start
  2.7 0.0 copy-done
  2.8 0.0 copy-done.1
  2.8 0.0 copy-start.3
  2.8 0.7 copy-done.3
  3.4 3.2 %shard_map.65 = f32[16,40,128]{2,1,0:T(8,128)S(1)} custom-call(bf16[64,2,512]{2,1,0:T(2,128)(2,1)S(1)} %copy-done.1, s32[64,512]{1,0:T(8,128)S(1)} %copy-done, f32[8,128]{1,0:T(8,128)S(1)} %copy-done.3), custom_call_target="tpu_custom_call" | custom-call | tf_op jit(solution)/shard_map/pallas_call | solution.py:217
  6.7 0.0 collective-permute-done
  6.7 21.2 %all_to_all.20.in_ref = f32[16,40,128]{2,1,0:T(8,128)S(1)} all-to-all(f32[16,40,128]{2,1,0:T(8,128)S(1)} %bitcast.8), channel_id=1, replica_groups=mesh['bunch'=8,'zq'=4,'z0'=2,'y'=8] {'z0','y'}, dimensions={0} | all-to-all | bytes 655360 | tf_op jit(solution)/shard_map/all_to_all | solution.py:190
  27.9 17.7 %all_to_all.21.in_ref = f32[4,40,128]{2,1,0:T(8,128)S(1)} all-to-all(f32[4,40,128]{2,1,0:T(8,128)S(1)} %shard_map.66), channel_id=1, replica_groups=mesh['bunch'=8,'zq'=4,'z0'=2,'y'=8] {'zq'}, dimensions={0} | all-to-all | bytes 163840 | tf_op jit(solution)/shard_map/all_to_all | solution.py:190
  45.6 13.7 %all_to_all.22.in_ref = bf16[16,48,128]{2,1,0:T(8,128)(2,1)S(1)} all-to-all(bf16[16,48,128]{2,1,0:T(8,128)(2,1)S(1)} %shard_map.67), channel_id=1, replica_groups=mesh['bunch'=8,'zq'=4,'z0'=2,'y'=8] {'z0','y'}, dimensions={0} | all-to-all | bytes 393216 | tf_op jit(solution)/shard_map/all_to_all | solution.py:190
  59.3 0.0 copy-done.2
  59.3 0.0 copy-done.4
  59.3 1.0 %shard_map.68 = bf16[64,8,128]{2,1,0:T(8,128)(2,1)S(1)} custom-call(bf16[16,48,128]{2,1,0:T(8,128)(2,1)S(1)} %all_to_all.22.in_ref, bf16[2,4,8,512]{3,2,1,0:T(8,128)(2,1)S(1)} %copy-done.2, s32[512]{0:T(512)S(1)} %copy-done.4), custom_call_target="tpu_custom_call" | custom-call | tf_op jit(solution)/shard_map/pallas_call | solution.py:229
  60.3 17.1 %all_to_all.23.kick_ref = bf16[64,8,128]{2,1,0:T(8,128)(2,1)S(1)} all-to-all(bf16[64,8,128]{2,1,0:T(8,128)(2,1)S(1)} %shard_map.68), channel_id=1, replica_groups=mesh['bunch'=8,'zq'=4,'z0'=2,'y'=8] {'zq','z0','y'}, dimensions={0} | all-to-all | bytes 262144 | tf_op jit(solution)/shard_map/all_to_all | solution.py:190
  77.4 1.1 %shard_map.69 = bf16[64,2,512]{2,1,0:T(2,128)(2,1)} custom-call(bf16[64,8,128]{2,1,0:T(8,128)(2,1)S(1)} %all_to_all.23.kick_ref, s32[64,512]{1,0:T(8,128)S(1)} %copy-done), custom_call_target="tpu_custom_call" | custom-call | tf_op jit(solution)/shard_map/pallas_call | solution.py:236
  (3 shorter events, 0.0 us)
Async XLA Ops:
  0.0 2.7 %copy-start = (s32[64,512]{1,0:T(8,128)S(1)}, s32[64,512]{1,0:T(8,128)}, u32[]{:S(2)}) copy-start(s32[64,512]{1,0:T(8,128)} %index_ref.3) | copy-start | bytes 393220
  0.0 2.7 %copy-start.1 = (bf16[64,2,512]{2,1,0:T(2,128)(2,1)S(1)}, bf16[64,2,512]{2,1,0:T(2,128)(2,1)}, u32[]{:S(2)}) copy-start(bf16[64,2,512]{2,1,0:T(2,128)(2,1)} %coords_ref.1) | copy-start | bytes 393220
  0.0 59.3 %copy-start.2 = (bf16[2,4,8,512]{3,2,1,0:T(8,128)(2,1)S(1)}, bf16[2,4,8,512]{3,2,1,0:T(8,128)(2,1)}, u32[]{:S(2)}) copy-start(bf16[2,4,8,512]{3,2,1,0:T(8,128)(2,1)} %panels_ref.1) | copy-start | bytes 196612
  0.0 59.3 %copy-start.4 = (s32[512]{0:T(512)S(1)}, s32[512]{0:T(512)}, u32[]{:S(2)}) copy-start(s32[512]{0:T(512)} %fill_ref.1) | copy-start | bytes 6148
  2.7 3.9 %collective-permute-start = (f32[8,8,128]{2,1,0:T(8,128)}, f32[8,8,128]{2,1,0:T(8,128)S(1)}, u32[]{:S(2)}, u32[]{:S(2)}) collective-permute-start(f32[8,8,128]{2,1,0:T(8,128)} %get-tuple-element.20), channel_id=1, source_target_pairs={{0,64},{64,128},{128,192},{192,256},{256,320},{320,384},{384,448},... | collective-permute-start | bytes 98312 | tf_op jit(solution)/shard_map/ppermute | solution.py:216
  2.8 0.7 copy-start.3

commit v3 on v2

--- a/solution.py
+++ b/solution.py
@@ -16,18 +16,19 @@
 COL4 = ("zq",)
 VMEM = pl.BlockSpec(memory_space=pltpu.VMEM)
 HBM = pl.BlockSpec(memory_space=pltpu.HBM)
-WIDE = pltpu.CompilerParams(vmem_limit_bytes=60 * 1024 * 1024)
 PARAMS = pltpu.CompilerParams(vmem_limit_bytes=32 * 1024 * 1024)
 
 
-def bunch_moment(coords_ref, index_ref, b):
+def lane_ids(count):
+    return lax.broadcasted_iota(jnp.int32, (LANES, count), 0).astype(F32).astype(BF16)
+
+
+def bunch_moment(coords_ref, index_ref, b, ids):
     count = index_ref.shape[1]
     row = index_ref[pl.ds(b, 1), :]
-    low = jnp.broadcast_to(row & (LANES - 1), (LANES, count))
+    low = jnp.broadcast_to((row & (LANES - 1)).astype(F32).astype(BF16), (LANES, count))
+    onehot = jnp.where(low == ids, jnp.ones((), BF16), jnp.zeros((), BF16))
     high = jnp.broadcast_to(row >> 7, (8, count))
-    onehot = jnp.where(
-        low == lax.broadcasted_iota(jnp.int32, (LANES, count), 0), 1.0, 0.0
-    ).astype(BF16)
     planes = coords_ref[b].astype(F32)
     sub = lax.broadcasted_iota(jnp.int32, (8, count), 0)
     both = jnp.where(sub < 4, planes[0:1], planes[1:2])
@@ -37,56 +38,67 @@
     )
 
 
+def add_past_turns(hist, coef_ref, rows, first):
+    plane_ids = lax.broadcasted_iota(jnp.int32, hist.shape[1:], 0)
+    total = jnp.zeros(hist.shape[1:], F32)
+    for turn in range(hist.shape[0]):
+        total = total + hist[turn] * jnp.where(plane_ids == 0, coef_ref[0, turn], coef_ref[1, turn])
+    parts = [
+        total[plane : plane + 1, high * LANES : (high + 1) * LANES]
+        for plane in range(2)
+        for high in range(4)
+    ]
+    at = pl.ds(pl.multiple_of(first, 8), 8)
+    rows[at, :] = rows[at, :] + jnp.concatenate(parts, 0)
+
+
 def halo_kernel(
-    scale, coords_hbm, index_hbm, hist_hbm, coef_ref, halo_ref, carried_ref, coords, index, hist, rows, sems
+    scale, coords_hbm, index_hbm, hist_hbm, coef_hbm, halo_ref, coords, index, hist, coef_ref, rows, sems
 ):
     dom = lax.axis_index(DOM)
     bunches = index_hbm.shape[0]
     last = pl.ds(bunches - 8, 8)
-    copies = [
-        pltpu.make_async_copy(index_hbm.at[last], index, sems.at[0]),
-        pltpu.make_async_copy(coords_hbm.at[last], coords, sems.at[1]),
-        pltpu.make_async_copy(hist_hbm.at[dom], hist, sems.at[2]),
-    ]
-    for copy in copies:
-        copy.start()
-    copies[0].wait()
-    copies[1].wait()
+    copy_index = pltpu.make_async_copy(index_hbm.at[last], index, sems.at[0])
+    copy_coords = pltpu.make_async_copy(coords_hbm.at[last], coords, sems.at[1])
+    copy_hist = pltpu.make_async_copy(hist_hbm.at[dom], hist, sems.at[2])
+    copy_coef = pltpu.make_async_copy(coef_hbm, coef_ref, sems.at[3])
+    copy_index.start()
+    copy_coords.start()
+    copy_hist.start()
+    copy_coef.start()
+    copy_index.wait()
+    copy_coords.wait()
+    ids = lane_ids(index.shape[1])
     for b in range(8):
-        rows[pl.ds(8 * b, 8), :] = scale * bunch_moment(coords, index, b)
-    copies[2].wait()
-    total = jnp.zeros(hist.shape[1:], F32)
-    for turn in range(hist.shape[0]):
-        for_turn = jnp.concatenate(
-            [jnp.full((1, 1), coef_ref[0, turn]), jnp.full((1, 1), coef_ref[1, turn])], 0
-        )
-        total = total + hist[turn] * for_turn
-    for plane in range(2):
-        for high in range(4):
-            carried_ref[pl.ds(plane * 4 + high, 1), :] = total[
-                plane : plane + 1, high * LANES : (high + 1) * LANES
-            ]
+        rows[pl.ds(8 * b, 8), :] = scale * bunch_moment(coords, index, b, ids)
+    copy_hist.wait()
+    copy_coef.wait()
 
     @pl.when(dom >= bunches - 8)
     def _():
-        at = pl.ds(pl.multiple_of((dom - (bunches - 8)) * 8, 8), 8)
-        rows[at, :] = rows[at, :] + carried_ref[...]
+        add_past_turns(hist, coef_ref, rows, (dom - (bunches - 8)) * 8)
 
     for ph in range(8):
         halo_ref[ph] = rows[pl.ds(ph, 8, stride=8), :]
 
 
-def moment_kernel(scale, coords_ref, index_ref, carried_ref, out_ref, rows):
+def moment_kernel(scale, coords_ref, index_ref, hist_hbm, coef_hbm, out_ref, hist, coef_ref, rows, sems):
     dom = lax.axis_index(DOM)
     bunches = index_ref.shape[0]
+    copy_hist = pltpu.make_async_copy(hist_hbm.at[dom], hist, sems.at[0])
+    copy_coef = pltpu.make_async_copy(coef_hbm, coef_ref, sems.at[1])
+    copy_hist.start()
+    copy_coef.start()
+    ids = lane_ids(index_ref.shape[1])
 
     def one(b, _):
-        rows[pl.ds(pl.multiple_of(8 * b, 8), 8), :] = scale * bunch_moment(coords_ref, index_ref, b)
+        rows[pl.ds(pl.multiple_of(8 * b, 8), 8), :] = scale * bunch_moment(coords_ref, index_ref, b, ids)
         return 0
 
     lax.fori_loop(0, bunches, one, 0, unroll=8)
-    at = pl.ds(pl.multiple_of(dom * 8, 8), 8)
-    rows[at, :] = rows[at, :] + carried_ref[...]
+    copy_hist.wait()
+    copy_coef.wait()
+    add_past_turns(hist, coef_ref, rows, dom * 8)
     for ph in range(8):
         for half in range(2):
             for tile in range(4):
@@ -175,14 +187,14 @@
             out_ref[pl.ds(block * 8, 8), :, pl.ds(tile * LANES, LANES)] = jnp.stack(found, 1).astype(BF16)
 
 
-def call(kernel, out_shape, in_specs, scratch=(), out_specs=None, params=PARAMS):
+def call(kernel, out_shape, in_specs, scratch=()):
     return pl.pallas_call(
         kernel,
         out_shape=out_shape,
         in_specs=in_specs,
-        out_specs=VMEM if out_specs is None else out_specs,
+        out_specs=VMEM,
         scratch_shapes=list(scratch),
-        compiler_params=params,
+        compiler_params=PARAMS,
     )
 
 
@@ -198,28 +210,35 @@
     shape = jax.ShapeDtypeStruct
     smem = pl.BlockSpec(memory_space=pltpu.SMEM)
 
-    halo, carried = call(
+    far = pltpu.with_memory_space_constraint
+    coef = far(turn_coef.T, pltpu.HBM)
+    past = far(history, pltpu.HBM)
+    halo = call(
         functools.partial(halo_kernel, scale),
-        (shape((8, 8, LANES), F32), shape((8, LANES), F32)),
-        [HBM, HBM, HBM, smem],
+        pltpu.VMEM((8, 8, LANES), F32),
+        [HBM, HBM, HBM, HBM],
         [
             pltpu.VMEM((8, 2, count), BF16),
             pltpu.VMEM((8, count), jnp.int32),
             pltpu.VMEM((turns, 2, slices), F32),
+            pltpu.SMEM((2, turns), F32),
             pltpu.VMEM((64, LANES), F32),
-            pltpu.SemaphoreType.DMA((3,)),
+            pltpu.SemaphoreType.DMA((4,)),
         ],
-        (VMEM, VMEM),
-        WIDE,
-    )(coords, slice_index, history, turn_coef.T)
+    )(far(coords, pltpu.HBM), far(slice_index, pltpu.HBM), past, coef)
     ring = lax.axis_size("bunch")
     halo = lax.ppermute(halo, "bunch", [(i, (i + 1) % ring) for i in range(ring)])
     partial = call(
         functools.partial(moment_kernel, scale),
         shape((16, 40, LANES), F32),
-        [VMEM, VMEM, VMEM],
-        [pltpu.VMEM((bunches * 8, LANES), F32)],
-    )(coords, slice_index, carried)
+        [VMEM, VMEM, HBM, HBM],
+        [
+            pltpu.VMEM((turns, 2, slices), F32),
+            pltpu.SMEM((2, turns), F32),
+            pltpu.VMEM((bunches * 8, LANES), F32),
+            pltpu.SemaphoreType.DMA((2,)),
+        ],
+    )(coords, slice_index, past, coef)
     partial = partial.reshape(8, 2, 40, LANES).at[:, 0, 0:8].set(halo).reshape(16, 40, LANES)
     part = exchange(partial, ROW16)
     part = call(sum_kernel, shape((4, 40, LANES), F32), [VMEM])(part)

time: 78.9 us -> 76.8 us (0.973)
  the two profiles are of different devices: /device:TPU:4 before, /device:TPU:2 now
where the time goes in v3:
time: 76.8 us; the launch traced here: 76.5 us
  blocking collectives  69.6 us (91%)
  Pallas kernels  6.72 us (9%)
    all_to_all x4, blocking collectives, exchange(): return lax.all_to_all(value, axes, 0, 0, tiled=True)  69.6 us
    pallas_call x1, Pallas kernels, local(): call(functools.partial(moment_kernel, scale), shape((16, 40, LANES), F32)...  3.3 us
  transfers between devices with their start and end apart: 1, of which 0 were waited for; matrix products, arithmetic and copies ran while one was open for 0% of the time, Pallas kernels for 4%

profile of v3, /device:TPU:2, one launch (start us, length us, event | category | flops | bytes accessed | tf_op | source)
XLA Modules:
  0.0 76.5 jit_solution(17002259364870994648)
XLA Ops:
  0.0 0.0 copy-start
  0.0 0.0 copy-start.1
  0.0 1.2 %shard_map.65 = f32[8,8,128]{2,1,0:T(8,128)S(1)} custom-call(bf16[64,2,512]{2,1,0:T(2,128)(2,1)} %coords_hbm.1, s32[64,512]{1,0:T(8,128)} %index_ref.3, f32[64,16,2,512]{3,2,1,0:T(2,128)} %hist_hbm.3, f32[2,16]{1,0:T(2,128)} %bitcast.9), custom_call_target="tpu_custom_call" | custom-call | tf_op jit(solution)/shard_map/pallas_call | solution.py:216
  1.3 0.0 copy-start.2
  1.3 0.0 copy-start.3
  1.3 0.0 collective-permute-start
  1.3 0.0 copy-done
  1.3 0.0 copy-done.1
  1.3 3.3 %shard_map.64 = f32[16,40,128]{2,1,0:T(8,128)S(1)} custom-call(bf16[64,2,512]{2,1,0:T(2,128)(2,1)S(1)} %copy-done.1, s32[64,512]{1,0:T(8,128)S(1)} %copy-done, f32[64,16,2,512]{3,2,1,0:T(2,128)} %hist_hbm.3, f32[2,16]{1,0:T(2,128)} %bitcast.10), custom_call_target="tpu_custom_call" | custom-call | tf_op jit(solution)/shard_map/pallas_call | solution.py:231
  4.6 0.0 collective-permute-done
  4.6 20.9 %all_to_all.20.in_ref = f32[16,40,128]{2,1,0:T(8,128)S(1)} all-to-all(f32[16,40,128]{2,1,0:T(8,128)S(1)} %bitcast.8), channel_id=1, replica_groups=mesh['bunch'=8,'zq'=4,'z0'=2,'y'=8] {'z0','y'}, dimensions={0} | all-to-all | bytes 655360 | tf_op jit(solution)/shard_map/all_to_all | solution.py:202
  25.5 17.8 %all_to_all.21.in_ref = f32[4,40,128]{2,1,0:T(8,128)S(1)} all-to-all(f32[4,40,128]{2,1,0:T(8,128)S(1)} %shard_map.66), channel_id=1, replica_groups=mesh['bunch'=8,'zq'=4,'z0'=2,'y'=8] {'zq'}, dimensions={0} | all-to-all | bytes 163840 | tf_op jit(solution)/shard_map/all_to_all | solution.py:202
  43.4 13.8 %all_to_all.22.in_ref = bf16[16,48,128]{2,1,0:T(8,128)(2,1)S(1)} all-to-all(bf16[16,48,128]{2,1,0:T(8,128)(2,1)S(1)} %shard_map.67), channel_id=1, replica_groups=mesh['bunch'=8,'zq'=4,'z0'=2,'y'=8] {'z0','y'}, dimensions={0} | all-to-all | bytes 393216 | tf_op jit(solution)/shard_map/all_to_all | solution.py:202
  57.2 0.0 copy-done.2
  57.2 0.0 copy-done.3
  57.2 1.0 %shard_map.68 = bf16[64,8,128]{2,1,0:T(8,128)(2,1)S(1)} custom-call(bf16[16,48,128]{2,1,0:T(8,128)(2,1)S(1)} %all_to_all.22.in_ref, bf16[2,4,8,512]{3,2,1,0:T(8,128)(2,1)S(1)} %copy-done.2, s32[512]{0:T(512)S(1)} %copy-done.3), custom_call_target="tpu_custom_call" | custom-call | tf_op jit(solution)/shard_map/pallas_call | solution.py:248
  58.3 17.1 %all_to_all.23.kick_ref = bf16[64,8,128]{2,1,0:T(8,128)(2,1)S(1)} all-to-all(bf16[64,8,128]{2,1,0:T(8,128)(2,1)S(1)} %shard_map.68), channel_id=1, replica_groups=mesh['bunch'=8,'zq'=4,'z0'=2,'y'=8] {'zq','z0','y'}, dimensions={0} | all-to-all | bytes 262144 | tf_op jit(solution)/shard_map/all_to_all | solution.py:202
  75.4 1.1 %shard_map.69 = bf16[64,2,512]{2,1,0:T(2,128)(2,1)} custom-call(bf16[64,8,128]{2,1,0:T(8,128)(2,1)S(1)} %all_to_all.23.kick_ref, s32[64,512]{1,0:T(8,128)S(1)} %copy-done), custom_call_target="tpu_custom_call" | custom-call | tf_op jit(solution)/shard_map/pallas_call | solution.py:255
  (3 shorter events, 0.0 us)
Async XLA Ops:
  0.0 1.3 %copy-start = (s32[64,512]{1,0:T(8,128)S(1)}, s32[64,512]{1,0:T(8,128)}, u32[]{:S(2)}) copy-start(s32[64,512]{1,0:T(8,128)} %index_ref.3) | copy-start | bytes 393220
  0.0 1.3 %copy-start.1 = (bf16[64,2,512]{2,1,0:T(2,128)(2,1)S(1)}, bf16[64,2,512]{2,1,0:T(2,128)(2,1)}, u32[]{:S(2)}) copy-start(bf16[64,2,512]{2,1,0:T(2,128)(2,1)} %coords_hbm.1) | copy-start | bytes 393220
  1.3 56.0 %copy-start.2 = (bf16[2,4,8,512]{3,2,1,0:T(8,128)(2,1)S(1)}, bf16[2,4,8,512]{3,2,1,0:T(8,128)(2,1)}, u32[]{:S(2)}) copy-start(bf16[2,4,8,512]{3,2,1,0:T(8,128)(2,1)} %panels_ref.1) | copy-start | bytes 196612
  1.3 56.0 %copy-start.3 = (s32[512]{0:T(512)S(1)}, s32[512]{0:T(512)}, u32[]{:S(2)}) copy-start(s32[512]{0:T(512)} %fill_ref.1) | copy-start | bytes 6148
  1.3 3.4 %collective-permute-start = (f32[8,8,128]{2,1,0:T(8,128)S(1)}, f32[8,8,128]{2,1,0:T(8,128)S(1)}, u32[]{:S(2)}, u32[]{:S(2)}) collective-permute-start(f32[8,8,128]{2,1,0:T(8,128)S(1)} %shard_map.65), channel_id=1, source_target_pairs={{0,64},{64,128},{128,192},{192,256},{256,320},{320,384},{384,448},... | collective-permute-start | bytes 98312 | tf_op jit(solution)/shard_map/ppermute | solution.py:230

commit v4 on v3

--- a/solution.py
+++ b/solution.py
@@ -13,7 +13,7 @@
 LANES = 128
 DOM = ("zq", "z0", "y")
 ROW16 = ("z0", "y")
-COL4 = ("zq",)
+COL8 = ("zq", "z0")
 VMEM = pl.BlockSpec(memory_space=pltpu.VMEM)
 HBM = pl.BlockSpec(memory_space=pltpu.HBM)
 PARAMS = pltpu.CompilerParams(vmem_limit_bytes=32 * 1024 * 1024)
@@ -79,7 +79,7 @@
         add_past_turns(hist, coef_ref, rows, (dom - (bunches - 8)) * 8)
 
     for ph in range(8):
-        halo_ref[ph] = rows[pl.ds(ph, 8, stride=8), :]
+        halo_ref[ph // 4, pl.ds((ph % 4) * 4, 4), :] = rows[pl.ds(32 + ph, 4, stride=8), :]
 
 
 def moment_kernel(scale, coords_ref, index_ref, hist_hbm, coef_hbm, out_ref, hist, coef_ref, rows, sems):
@@ -99,13 +99,22 @@
     copy_hist.wait()
     copy_coef.wait()
     add_past_turns(hist, coef_ref, rows, dom * 8)
-    for ph in range(8):
-        for half in range(2):
-            for tile in range(4):
-                first = (half * 32 + tile * 8) * 8
-                out_ref[ph * 2 + half, pl.ds(8 + tile * 8, 8), :] = rows[pl.ds(first + ph, 8, stride=8), :]
-            if half == 1:
-                out_ref[ph * 2 + half, pl.ds(0, 8), :] = jnp.zeros((8, LANES), F32)
+    for group in range(8):
+        for ph in range(8):
+            chunk, high = (ph // 4) * 8 + group, ph % 4
+            if group > 0:
+                out_ref[chunk, pl.ds(high * 4, 4), :] = rows[pl.ds((group * 8 - 4) * 8 + ph, 4, stride=8), :]
+            out_ref[chunk, pl.ds(16 + high * 8, 8), :] = rows[pl.ds(group * 64 + ph, 8, stride=8), :]
+
+
+def pair_kernel(bit, mine_ref, got_ref, both_ref):
+    place_panels(bit, mine_ref, got_ref, both_ref)
+
+
+def place_panels(bit, mine_ref, got_ref, both_ref):
+    upper = (lax.axis_index("y") >> bit) & 1
+    both_ref[upper] = mine_ref[...]
+    both_ref[1 - upper] = got_ref[...]
 
 
 def sum_kernel(in_ref, out_ref):
@@ -116,48 +125,45 @@
         out_ref[copy] = total
 
 
-def source_kernel(in_ref, out_ref):
-    total = in_ref[0]
-    for part in range(1, in_ref.shape[0]):
-        total = total + in_ref[part]
-    total = jnp.concatenate([total, jnp.zeros((8, LANES), F32)], 0).astype(BF16)
-    for copy in range(out_ref.shape[0]):
-        out_ref[copy] = total
-
-
-def kick_kernel(total_bunches, in_ref, panels_ref, fill_ref, out_ref, source, bucket):
-    bunches = 64
-    first = lax.axis_index("bunch") * bunches
+def kick_kernel(total_bunches, bit, in_ref, mine_ref, got_ref, fill_ref, out_ref, source, bucket, wide):
+    first = lax.axis_index("bunch") * 64 + lax.axis_index("y") * 8 - 4 + total_bunches
     sub = lax.broadcasted_iota(jnp.int32, (8, LANES), 0)
-    for tile in range(9):
+    for tile in range(2):
         column = jnp.zeros((8, LANES), jnp.int32)
-        for row in range(8):
-            place = first - 8 + tile * 8 + row + total_bunches
+        for row in range(8 if tile == 0 else 4):
+            place = first + tile * 8 + row
             place = jnp.where(place >= total_bunches, place - total_bunches, place)
             column = jnp.where(sub == row, fill_ref[place], column)
         bucket[pl.ds(tile * 8, 8), :] = column
-    for ph in range(8):
-        source[ph, pl.ds(0, 40), :] = in_ref[2 * ph].astype(F32)[0:40]
-        source[ph, pl.ds(40, 32), :] = in_ref[2 * ph + 1].astype(F32)[8:40]
+    place_panels(bit, mine_ref, got_ref, wide)
+    for plane in range(2):
+        total = in_ref[plane]
+        for part in range(1, in_ref.shape[0] // 2):
+            total = total + in_ref[2 * part + plane]
+        total = total.astype(BF16).astype(F32)
+        for high in range(4):
+            source[plane, high, pl.ds(4, 4), :] = total[high * 4 : high * 4 + 4]
+            source[plane, high, pl.ds(8, 8), :] = total[16 + high * 8 : 24 + high * 8]
     cycle = 2 * total_bunches
-    here = bucket[pl.ds(8, bunches), :]
-    gaps = [None] + [(here - bucket[pl.ds(8 - d, bunches), :]) & (cycle - 1) for d in (1, 2, 3)]
+    here = bucket[pl.ds(4, 8), :]
+    gaps = [None] + [(here - bucket[pl.ds(4 - d, 8), :]) & (cycle - 1) for d in (1, 2, 3)]
     outs = []
     for plane in range(2):
         picked = [[], [], [], []]
         for high in range(4):
-            ph = plane * 4 + high
-            past = [source[ph, pl.ds(8 - d, bunches), :] for d in range(4)]
-            picked[0].append(past[0].astype(BF16))
+            past = [source[plane, high, pl.ds(8 - d, 8), :] for d in range(4)]
+            picked[0].append(past[0])
             for k in (1, 2, 3):
-                value = jnp.zeros((bunches, LANES), F32)
+                value = jnp.zeros((8, LANES), F32)
                 for d in range(1, k + 1):
                     value = jnp.where(gaps[d] == k, past[d], value)
-                picked[k].append(value.astype(BF16))
+                picked[k].append(value)
         total = None
         for k in range(4):
-            right = jnp.concatenate(picked[k], 1)
-            left = panels_ref[plane, k]
+            left = jnp.concatenate(picked[k], 1).astype(BF16)
+            right = jnp.concatenate(
+                [wide[y // 4, (y // 2) % 2, y % 2, plane, k].astype(F32) for y in range(8)], 0
+            ).astype(BF16)
             part = lax.dot_general(left, right, (((1,), (1,)), ((), ())), preferred_element_type=F32)
             total = part if total is None else total + part
         outs.append(total)
@@ -166,12 +172,17 @@
         out_ref[copy] = kick
 
 
-def lookup_kernel(kick_ref, index_ref, out_ref, table):
+def lookup_kernel(kick_ref, index_ref, out_ref):
     bunches = index_ref.shape[0]
-    for high in range(4):
-        rows = jnp.concatenate([kick_ref[16 * high + part].astype(F32) for part in range(16)], 0)
-        table[high] = rows.T
+    half = LANES // 2
+    lower = lax.broadcasted_iota(jnp.int32, (8, LANES), 1) < half
     for block in range(bunches // 8):
+        table = [[], []]
+        for high in range(4):
+            first = kick_ref[2 * high * 8 + block].astype(F32)
+            second = kick_ref[(2 * high + 1) * 8 + block].astype(F32)
+            table[0].append(jnp.where(lower, first, pltpu.roll(second, half, 1)))
+            table[1].append(jnp.where(lower, pltpu.roll(first, half, 1), second))
         for tile in range(index_ref.shape[1] // LANES):
             index = index_ref[pl.ds(block * 8, 8), pl.ds(tile * LANES, LANES)]
             low = index & (LANES - 1)
@@ -180,8 +191,7 @@
             for plane in range(2):
                 value = None
                 for high in range(4):
-                    row = table[high, pl.ds(plane * bunches + block * 8, 8), :]
-                    got = jnp.take_along_axis(row, low, axis=1)
+                    got = jnp.take_along_axis(table[plane][high], low, axis=1)
                     value = got if value is None else jnp.where(top == high, got, value)
                 found.append(value)
             out_ref[pl.ds(block * 8, 8), :, pl.ds(tile * LANES, LANES)] = jnp.stack(found, 1).astype(BF16)
@@ -198,6 +208,18 @@
     )
 
 
+def neighbour(value, bit):
+    return lax.ppermute(value, "y", [(i, i ^ (1 << bit)) for i in range(8)])
+
+
+def beside(bit, mine, got):
+    return call(
+        functools.partial(pair_kernel, bit),
+        jax.ShapeDtypeStruct((2, *mine.shape), BF16),
+        [VMEM, VMEM],
+    )(mine, got)
+
+
 def exchange(value, axes):
     return lax.all_to_all(value, axes, 0, 0, tiled=True)
 
@@ -215,7 +237,7 @@
     past = far(history, pltpu.HBM)
     halo = call(
         functools.partial(halo_kernel, scale),
-        pltpu.VMEM((8, 8, LANES), F32),
+        pltpu.VMEM((2, 16, LANES), F32),
         [HBM, HBM, HBM, HBM],
         [
             pltpu.VMEM((8, 2, count), BF16),
@@ -228,9 +250,10 @@
     )(far(coords, pltpu.HBM), far(slice_index, pltpu.HBM), past, coef)
     ring = lax.axis_size("bunch")
     halo = lax.ppermute(halo, "bunch", [(i, (i + 1) % ring) for i in range(ring)])
+    got = neighbour(panels, 0)
     partial = call(
         functools.partial(moment_kernel, scale),
-        shape((16, 40, LANES), F32),
+        shape((16, 48, LANES), F32),
         [VMEM, VMEM, HBM, HBM],
         [
             pltpu.VMEM((turns, 2, slices), F32),
@@ -239,25 +262,25 @@
             pltpu.SemaphoreType.DMA((2,)),
         ],
     )(coords, slice_index, past, coef)
-    partial = partial.reshape(8, 2, 40, LANES).at[:, 0, 0:8].set(halo).reshape(16, 40, LANES)
+    partial = partial.reshape(2, 8, 48, LANES).at[:, 0, 0:16].set(halo).reshape(16, 48, LANES)
     part = exchange(partial, ROW16)
-    part = call(sum_kernel, shape((4, 40, LANES), F32), [VMEM])(part)
-    part = exchange(part, COL4)
-    source = call(source_kernel, shape((16, 48, LANES), BF16), [VMEM])(part)
-    source = exchange(source, ROW16)
+    pair = beside(0, panels, got)
+    four = beside(1, pair, neighbour(pair, 1))
+    part = call(sum_kernel, shape((8, 48, LANES), F32), [VMEM])(part)
+    got = neighbour(four, 2)
+    part = exchange(part, COL8)
     kick = call(
-        functools.partial(kick_kernel, bunches * ring),
+        functools.partial(kick_kernel, bunches * ring, 2),
         shape((64, 8, LANES), BF16),
-        [VMEM, VMEM, smem],
-        [pltpu.VMEM((8, 72, LANES), F32), pltpu.VMEM((72, LANES), jnp.int32)],
-    )(source, panels, fill)
+        [VMEM, VMEM, VMEM, smem],
+        [
+            pltpu.VMEM((2, 4, 16, LANES), F32),
+            pltpu.VMEM((16, LANES), jnp.int32),
+            pltpu.VMEM((2, *four.shape), BF16),
+        ],
+    )(part, four, got, fill)
     kick = exchange(kick, DOM)
-    return call(
-        lookup_kernel,
-        shape((bunches, 2, count), BF16),
-        [VMEM, VMEM],
-        [pltpu.VMEM((4, LANES, LANES), F32)],
-    )(kick, slice_index)
+    return call(lookup_kernel, shape((bunches, 2, count), BF16), [VMEM, VMEM])(kick, slice_index)
 
 
 def solution(mesh):

time: 76.8 us -> 88.2 us (1.15)
  blocking collectives: 69.6 us -> 26.8 us
  starting transfers between devices: 0.02 us -> 31.4 us
  waiting for transfers between devices: 0.01 us -> 20.3 us
  Pallas kernels: 6.72 us -> 8.44 us
    all_to_all x4 -> x1, blocking collectives: 69.6 us -> 26.8 us  [exchange(): return lax.all_to_all(value, axes, 0, 0, tiled=True)]
    ppermute x0 -> x3, waiting for transfers between devices: none -> 20.3 us  [neighbour(): return lax.ppermute(value, 'y', [(i, i ^ 1 << bit) for i in range(8)])]
    all_to_all x0 -> x2, starting transfers between devices: none -> 18.4 us  [exchange(): return lax.all_to_all(value, axes, 0, 0, tiled=True)]
    ppermute x0 -> x3, starting transfers between devices: none -> 13 us  [neighbour(): return lax.ppermute(value, 'y', [(i, i ^ 1 << bit) for i in range(8)])]
    pallas_call x6 -> x7, Pallas kernels: 6.72 us -> 8.44 us  [the longest x1 4.05 us: local(): call(functools.partial(moment_kernel, scale), shape((16, 48, LANES), F32)...]
  transfers between devices with their start and end apart: 1 -> 6, of which waited for: 0 -> 2; matrix products, arithmetic and copies ran while one was open for 0% -> 0% of each run, Pallas kernels for 4% -> 5%
where the time goes in v4:
time: 88.2 us; the launch traced here: 87.8 us
  starting transfers between devices  31.4 us (36%)
  blocking collectives  26.8 us (30%)
  waiting for transfers between devices  20.3 us (23%)
  Pallas kernels  8.44 us (10%)
    all_to_all x1, blocking collectives, exchange(): return lax.all_to_all(value, axes, 0, 0, tiled=True)  26.8 us
    ppermute x3, waiting for transfers between devices, neighbour(): return lax.ppermute(value, 'y', [(i, i ^ 1 << bit) for i in range(8)])  20.3 us
    all_to_all x2, starting transfers between devices, exchange(): return lax.all_to_all(value, axes, 0, 0, tiled=True)  18.4 us
    ppermute x3, starting transfers between devices, neighbour(): return lax.ppermute(value, 'y', [(i, i ^ 1 << bit) for i in range(8)])  13 us
    pallas_call x1, Pallas kernels, local(): call(functools.partial(moment_kernel, scale), shape((16, 48, LANES), F32)...  4.05 us
  transfers between devices with their start and end apart: 6, of which 2 were waited for; matrix products, arithmetic and copies ran while one was open for 0% of the time, Pallas kernels for 5%

profile of v4, /device:TPU:2, one launch (start us, length us, event | category | flops | bytes accessed | tf_op | source)
XLA Modules:
  0.0 87.8 jit_solution(976448502535714799)
XLA Ops:
  0.0 0.0 copy-start.1
  0.0 0.0 copy-start
  0.0 0.0 copy-start.2
  0.0 1.2 %shard_map.65 = f32[2,16,128]{2,1,0:T(8,128)S(1)} custom-call(bf16[64,2,512]{2,1,0:T(2,128)(2,1)} %coords_hbm.1, s32[64,512]{1,0:T(8,128)} %index_ref.3, f32[64,16,2,512]{3,2,1,0:T(2,128)} %hist_hbm.3, f32[2,16]{1,0:T(2,128)} %bitcast.7), custom_call_target="tpu_custom_call" | custom-call | tf_op jit(solution)/shard_map/pallas_call | solution.py:238
  1.3 0.0 copy-start.3
  1.3 0.0 collective-permute-start
  1.3 0.0 copy-done.1
  1.3 0.0 copy-done
  1.3 4.1 %shard_map.64 = f32[16,48,128]{2,1,0:T(8,128)} custom-call(bf16[64,2,512]{2,1,0:T(2,128)(2,1)S(1)} %copy-done.1, s32[64,512]{1,0:T(8,128)S(1)} %copy-done, f32[64,16,2,512]{3,2,1,0:T(2,128)} %hist_hbm.3, f32[2,16]{1,0:T(2,128)} %bitcast.8), custom_call_target="tpu_custom_call" | custom-call | tf_op jit(solution)/shard_map/pallas_call | solution.py:254
  5.4 0.0 collective-permute-done
  5.4 0.6 bitcast_dynamic-update-slice_fusion
  6.0 9.0 %all-to-all-start = ((f32[16,48,128]{2,1,0:T(8,128)}), f32[16,48,128]{2,1,0:T(8,128)S(1)}, u32[]{:S(2)}, u32[]{:S(2)}) async-start(f32[16,48,128]{2,1,0:T(8,128)} %bitcast.4), calls=%async_computation | async-start | bytes 786432 | tf_op jit(solution)/shard_map/all_to_all | solution.py:224
  15.0 0.0 copy-done.2
  15.0 3.8 %collective-permute-start.1 = (bf16[2,4,8,512]{3,2,1,0:T(8,128)(2,1)S(1)}, bf16[2,4,8,512]{3,2,1,0:T(8,128)(2,1)S(1)}, u32[]{:S(2)}, u32[]{:S(2)}) collective-permute-start(bf16[2,4,8,512]{3,2,1,0:T(8,128)(2,1)S(1)} %copy-done.2), channel_id=1, source_target_pairs={{0,1},{1,0},{2,3},{3,2},{4,5},{5,4},{6,7},{7,6},{8,9},{9,8},{10,11... | collective-permute-start | bytes 196616 | tf_op jit(solution)/shard_map/ppermute | solution.py:212
  18.9 9.3 %collective-permute-done.1.got_ref = bf16[2,4,8,512]{3,2,1,0:T(8,128)(2,1)S(1)} collective-permute-done((bf16[2,4,8,512]{3,2,1,0:T(8,128)(2,1)S(1)}, bf16[2,4,8,512]{3,2,1,0:T(8,128)(2,1)S(1)}, u32[]{:S(2)}, u32[]{:S(2)}) %collective-permute-start.1) | collective-permute-done | bytes 65568 | tf_op jit(solution)/shard_map/ppermute | solution.py:212
  28.2 4.1 %collective-permute-start.2 = (bf16[2,2,4,8,512]{4,3,2,1,0:T(8,128)(2,1)S(1)}, bf16[2,2,4,8,512]{4,3,2,1,0:T(8,128)(2,1)S(1)}, u32[]{:S(2)}, u32[]{:S(2)}) collective-permute-start(bf16[2,2,4,8,512]{4,3,2,1,0:T(8,128)(2,1)S(1)} %shard_map.67.mine_ref), channel_id=1, source_target_pairs={{0,2},{1,3},{2,0},{3,1},{4,6},{5,7},{6,4},{7,5},{8,10},{9,11},{10,... | collective-permute-start | bytes 393224 | tf_op jit(solution)/shard_map/ppermute | solution.py:212
  32.4 0.0 all-to-all-done.in_ref
  32.4 0.7 shard_map.66
  33.1 9.4 %all-to-all-start.1 = ((f32[8,48,128]{2,1,0:T(8,128)}), f32[8,48,128]{2,1,0:T(8,128)S(1)}, u32[]{:S(2)}, u32[]{:S(2)}) async-start(f32[8,48,128]{2,1,0:T(8,128)} %shard_map.66), calls=%async_computation.1 | async-start | bytes 393216 | tf_op jit(solution)/shard_map/all_to_all | solution.py:224
  42.5 0.0 collective-permute-done.2.got_ref
  42.6 5.0 %collective-permute-start.3 = (bf16[2,2,2,4,8,512]{5,4,3,2,1,0:T(8,128)(2,1)S(1)}, bf16[2,2,2,4,8,512]{5,4,3,2,1,0:T(8,128)(2,1)S(1)}, u32[]{:S(2)}, u32[]{:S(2)}) collective-permute-start(bf16[2,2,2,4,8,512]{5,4,3,2,1,0:T(8,128)(2,1)S(1)} %shard_map.68.mine_ref), channel_id=1, source_target_pairs={{0,4},{1,5},{2,6},{3,7},{4,0},{5,1},{6,2},{7,3},{8,12},{9,13},{10,... | collective-permute-start | bytes 786440 | tf_op jit(solution)/shard_map/ppermute | solution.py:212
  47.6 11.0 %collective-permute-done.3.got_ref = bf16[2,2,2,4,8,512]{5,4,3,2,1,0:T(8,128)(2,1)S(1)} collective-permute-done((bf16[2,2,2,4,8,512]{5,4,3,2,1,0:T(8,128)(2,1)S(1)}, bf16[2,2,2,4,8,512]{5,4,3,2,1,0:T(8,128)(2,1)S(1)}, u32[]{:S(2)}, u32[]{:S(2)}) %collective-permute-start.3) | collective-permute-done | bytes 262176 | tf_op jit(solution)/shard_map/ppermute | solution.py:212
  58.5 0.0 all-to-all-done.1.in_ref
  58.5 0.0 copy-done.3
  58.5 0.9 %shard_map.69 = bf16[64,8,128]{2,1,0:T(8,128)(2,1)S(1)} custom-call(f32[8,48,128]{2,1,0:T(8,128)S(1)} %all-to-all-done.1.in_ref, bf16[2,2,2,4,8,512]{5,4,3,2,1,0:T(8,128)(2,1)S(1)} %shard_map.68.mine_ref, bf16[2,2,2,4,8,512]{5,4,3,2,1,0:T(8,128)(2,1)S(1)} %collective-permute-done.3.got_ref, s32[512]{0:T(512)S(1)} %copy-done.3), custom_call_target="tpu_custom_call" | custom-call | tf_op jit(solution)/shard_map/pallas_call | solution.py:272
  59.5 26.8 %all_to_all.15.kick_ref = bf16[64,8,128]{2,1,0:T(8,128)(2,1)S(1)} all-to-all(bf16[64,8,128]{2,1,0:T(8,128)(2,1)S(1)} %shard_map.69), channel_id=1, replica_groups=mesh['bunch'=8,'zq'=4,'z0'=2,'y'=8] {'zq','z0','y'}, dimensions={0} | all-to-all | bytes 262144 | tf_op jit(solution)/shard_map/all_to_all | solution.py:224
  86.3 1.5 %shard_map.70 = bf16[64,2,512]{2,1,0:T(2,128)(2,1)} custom-call(bf16[64,8,128]{2,1,0:T(8,128)(2,1)S(1)} %all_to_all.15.kick_ref, s32[64,512]{1,0:T(8,128)S(1)} %copy-done), custom_call_target="tpu_custom_call" | custom-call | tf_op jit(solution)/shard_map/pallas_call | solution.py:283
  (2 shorter events, 0.0 us)
Async XLA Ops:
  0.0 1.3 %copy-start.1 = (bf16[64,2,512]{2,1,0:T(2,128)(2,1)S(1)}, bf16[64,2,512]{2,1,0:T(2,128)(2,1)}, u32[]{:S(2)}) copy-start(bf16[64,2,512]{2,1,0:T(2,128)(2,1)} %coords_hbm.1) | copy-start | bytes 393220
  0.0 1.3 %copy-start = (s32[64,512]{1,0:T(8,128)S(1)}, s32[64,512]{1,0:T(8,128)}, u32[]{:S(2)}) copy-start(s32[64,512]{1,0:T(8,128)} %index_ref.3) | copy-start | bytes 393220
  0.0 15.0 %copy-start.2 = (bf16[2,4,8,512]{3,2,1,0:T(8,128)(2,1)S(1)}, bf16[2,4,8,512]{3,2,1,0:T(8,128)(2,1)}, u32[]{:S(2)}) copy-start(bf16[2,4,8,512]{3,2,1,0:T(8,128)(2,1)} %mine_ref.1) | copy-start | bytes 196612
  1.3 57.3 %copy-start.3 = (s32[512]{0:T(512)S(1)}, s32[512]{0:T(512)}, u32[]{:S(2)}) copy-start(s32[512]{0:T(512)} %fill_ref.1) | copy-start | bytes 6148
  1.3 4.1 %collective-permute-start = (f32[2,16,128]{2,1,0:T(8,128)S(1)}, f32[2,16,128]{2,1,0:T(8,128)S(1)}, u32[]{:S(2)}, u32[]{:S(2)}) collective-permute-start(f32[2,16,128]{2,1,0:T(8,128)S(1)} %shard_map.65), channel_id=1, source_target_pairs={{0,64},{64,128},{128,192},{192,256},{256,320},{320,384},{384,448},... | collective-permute-start | bytes 49160 | tf_op jit(solution)/shard_map/ppermute | solution.py:252
  6.0 26.4 %all-to-all-start = ((f32[16,48,128]{2,1,0:T(8,128)}), f32[16,48,128]{2,1,0:T(8,128)S(1)}, u32[]{:S(2)}, u32[]{:S(2)}) async-start(f32[16,48,128]{2,1,0:T(8,128)} %bitcast.4), calls=%async_computation | async-start | bytes 786432 | tf_op jit(solution)/shard_map/all_to_all | solution.py:224
  15.0 13.2 %collective-permute-start.1 = (bf16[2,4,8,512]{3,2,1,0:T(8,128)(2,1)S(1)}, bf16[2,4,8,512]{3,2,1,0:T(8,128)(2,1)S(1)}, u32[]{:S(2)}, u32[]{:S(2)}) collective-permute-start(bf16[2,4,8,512]{3,2,1,0:T(8,128)(2,1)S(1)} %copy-done.2), channel_id=1, source_target_pairs={{0,1},{1,0},{2,3},{3,2},{4,5},{5,4},{6,7},{7,6},{8,9},{9,8},{10,11... | collective-permute-start | bytes 196616 | tf_op jit(solution)/shard_map/ppermute | solution.py:212
  28.2 14.3 %collective-permute-start.2 = (bf16[2,2,4,8,512]{4,3,2,1,0:T(8,128)(2,1)S(1)}, bf16[2,2,4,8,512]{4,3,2,1,0:T(8,128)(2,1)S(1)}, u32[]{:S(2)}, u32[]{:S(2)}) collective-permute-start(bf16[2,2,4,8,512]{4,3,2,1,0:T(8,128)(2,1)S(1)} %shard_map.67.mine_ref), channel_id=1, source_target_pairs={{0,2},{1,3},{2,0},{3,1},{4,6},{5,7},{6,4},{7,5},{8,10},{9,11},{10,... | collective-permute-start | bytes 393224 | tf_op jit(solution)/shard_map/ppermute | solution.py:212
  33.1 25.5 %all-to-all-start.1 = ((f32[8,48,128]{2,1,0:T(8,128)}), f32[8,48,128]{2,1,0:T(8,128)S(1)}, u32[]{:S(2)}, u32[]{:S(2)}) async-start(f32[8,48,128]{2,1,0:T(8,128)} %shard_map.66), calls=%async_computation.1 | async-start | bytes 393216 | tf_op jit(solution)/shard_map/all_to_all | solution.py:224
  42.6 16.0 %collective-permute-start.3 = (bf16[2,2,2,4,8,512]{5,4,3,2,1,0:T(8,128)(2,1)S(1)}, bf16[2,2,2,4,8,512]{5,4,3,2,1,0:T(8,128)(2,1)S(1)}, u32[]{:S(2)}, u32[]{:S(2)}) collective-permute-start(bf16[2,2,2,4,8,512]{5,4,3,2,1,0:T(8,128)(2,1)S(1)} %shard_map.68.mine_ref), channel_id=1, source_target_pairs={{0,4},{1,5},{2,6},{3,7},{4,0},{5,1},{6,2},{7,3},{8,12},{9,13},{10,... | collective-permute-start | bytes 786440 | tf_op jit(solution)/shard_map/ppermute | solution.py:212

commit v5 on v3

--- a/solution.py
+++ b/solution.py
@@ -79,7 +79,7 @@
         add_past_turns(hist, coef_ref, rows, (dom - (bunches - 8)) * 8)
 
     for ph in range(8):
-        halo_ref[ph] = rows[pl.ds(ph, 8, stride=8), :]
+        halo_ref[ph] = rows[pl.ds(ph, 8, stride=8), :].astype(BF16)
 
 
 def moment_kernel(scale, coords_ref, index_ref, hist_hbm, coef_hbm, out_ref, hist, coef_ref, rows, sems):
@@ -99,21 +99,19 @@
     copy_hist.wait()
     copy_coef.wait()
     add_past_turns(hist, coef_ref, rows, dom * 8)
+    blank = jnp.zeros((8, LANES), F32)
     for ph in range(8):
         for half in range(2):
-            for tile in range(4):
-                first = (half * 32 + tile * 8) * 8
-                out_ref[ph * 2 + half, pl.ds(8 + tile * 8, 8), :] = rows[pl.ds(first + ph, 8, stride=8), :]
-            if half == 1:
-                out_ref[ph * 2 + half, pl.ds(0, 8), :] = jnp.zeros((8, LANES), F32)
+            own = [rows[pl.ds((half * 32 + tile * 8) * 8 + ph, 8, stride=8), :] for tile in range(4)]
+            out_ref[ph * 2 + half] = jnp.concatenate([blank, *own, blank], 0).astype(BF16)
 
 
 def sum_kernel(in_ref, out_ref):
-    total = in_ref[0]
+    total = in_ref[0].astype(F32)
     for part in range(1, in_ref.shape[0]):
-        total = total + in_ref[part]
+        total = total + in_ref[part].astype(F32)
     for copy in range(out_ref.shape[0]):
-        out_ref[copy] = total
+        out_ref[copy] = total[0:40]
 
 
 def source_kernel(in_ref, out_ref):
@@ -215,7 +213,7 @@
     past = far(history, pltpu.HBM)
     halo = call(
         functools.partial(halo_kernel, scale),
-        pltpu.VMEM((8, 8, LANES), F32),
+        pltpu.VMEM((8, 8, LANES), BF16),
         [HBM, HBM, HBM, HBM],
         [
             pltpu.VMEM((8, 2, count), BF16),
@@ -230,7 +228,7 @@
     halo = lax.ppermute(halo, "bunch", [(i, (i + 1) % ring) for i in range(ring)])
     partial = call(
         functools.partial(moment_kernel, scale),
-        shape((16, 40, LANES), F32),
+        shape((16, 48, LANES), BF16),
         [VMEM, VMEM, HBM, HBM],
         [
             pltpu.VMEM((turns, 2, slices), F32),
@@ -239,7 +237,7 @@
             pltpu.SemaphoreType.DMA((2,)),
         ],
     )(coords, slice_index, past, coef)
-    partial = partial.reshape(8, 2, 40, LANES).at[:, 0, 0:8].set(halo).reshape(16, 40, LANES)
+    partial = partial.reshape(8, 2, 48, LANES).at[:, 0, 0:8].set(halo).reshape(16, 48, LANES)
     part = exchange(partial, ROW16)
     part = call(sum_kernel, shape((4, 40, LANES), F32), [VMEM])(part)
     part = exchange(part, COL4)

time: 76.8 us -> 74.3 us (0.967)
  blocking collectives: 69.6 us -> 67.2 us
    all_to_all x4, blocking collectives: 69.6 us -> 67.2 us  [exchange(): return lax.all_to_all(value, axes, 0, 0, tiled=True)]
where the time goes in v5:
time: 74.3 us; the launch traced here: 74 us
  blocking collectives  67.2 us (90%)
  Pallas kernels  6.71 us (9%)
    all_to_all x4, blocking collectives, exchange(): return lax.all_to_all(value, axes, 0, 0, tiled=True)  67.2 us
    pallas_call x1, Pallas kernels, local(): call(functools.partial(moment_kernel, scale), shape((16, 48, LANES), BF16...  3.29 us
  transfers between devices with their start and end apart: 1, of which 0 were waited for; matrix products, arithmetic and copies ran while one was open for 0% of the time, Pallas kernels for 4%

profile of v5, /device:TPU:2, one launch (start us, length us, event | category | flops | bytes accessed | tf_op | source)
XLA Modules:
  0.0 74.0 jit_solution(9880636440059388069)
XLA Ops:
  0.0 0.0 copy-start
  0.0 0.0 copy-start.1
  0.0 1.2 %shard_map.65 = bf16[8,8,128]{2,1,0:T(8,128)(2,1)S(1)} custom-call(bf16[64,2,512]{2,1,0:T(2,128)(2,1)} %coords_hbm.1, s32[64,512]{1,0:T(8,128)} %index_ref.3, f32[64,16,2,512]{3,2,1,0:T(2,128)} %hist_hbm.3, f32[2,16]{1,0:T(2,128)} %bitcast.9), custom_call_target="tpu_custom_call" | custom-call | tf_op jit(solution)/shard_map/pallas_call | solution.py:214
  1.3 0.0 copy-start.2
  1.3 0.0 copy-start.3
  1.3 0.0 collective-permute-start
  1.3 0.0 copy-done
  1.3 0.0 copy-done.1
  1.3 3.3 %shard_map.64 = bf16[16,48,128]{2,1,0:T(8,128)(2,1)S(1)} custom-call(bf16[64,2,512]{2,1,0:T(2,128)(2,1)S(1)} %copy-done.1, s32[64,512]{1,0:T(8,128)S(1)} %copy-done, f32[64,16,2,512]{3,2,1,0:T(2,128)} %hist_hbm.3, f32[2,16]{1,0:T(2,128)} %bitcast.10), custom_call_target="tpu_custom_call" | custom-call | tf_op jit(solution)/shard_map/pallas_call | solution.py:229
  4.6 0.0 collective-permute-done
  4.6 18.4 %all_to_all.20.in_ref = bf16[16,48,128]{2,1,0:T(8,128)(2,1)S(1)} all-to-all(bf16[16,48,128]{2,1,0:T(8,128)(2,1)S(1)} %bitcast.8), channel_id=1, replica_groups=mesh['bunch'=8,'zq'=4,'z0'=2,'y'=8] {'z0','y'}, dimensions={0} | all-to-all | bytes 393216 | tf_op jit(solution)/shard_map/all_to_all | solution.py:200
  23.1 17.7 %all_to_all.21.in_ref = f32[4,40,128]{2,1,0:T(8,128)S(1)} all-to-all(f32[4,40,128]{2,1,0:T(8,128)S(1)} %shard_map.66), channel_id=1, replica_groups=mesh['bunch'=8,'zq'=4,'z0'=2,'y'=8] {'zq'}, dimensions={0} | all-to-all | bytes 163840 | tf_op jit(solution)/shard_map/all_to_all | solution.py:200
  40.8 13.5 %all_to_all.22.in_ref = bf16[16,48,128]{2,1,0:T(8,128)(2,1)S(1)} all-to-all(bf16[16,48,128]{2,1,0:T(8,128)(2,1)S(1)} %shard_map.67), channel_id=1, replica_groups=mesh['bunch'=8,'zq'=4,'z0'=2,'y'=8] {'z0','y'}, dimensions={0} | all-to-all | bytes 393216 | tf_op jit(solution)/shard_map/all_to_all | solution.py:200
  54.4 0.0 copy-done.2
  54.4 0.0 copy-done.3
  54.4 1.0 %shard_map.68 = bf16[64,8,128]{2,1,0:T(8,128)(2,1)S(1)} custom-call(bf16[16,48,128]{2,1,0:T(8,128)(2,1)S(1)} %all_to_all.22.in_ref, bf16[2,4,8,512]{3,2,1,0:T(8,128)(2,1)S(1)} %copy-done.2, s32[512]{0:T(512)S(1)} %copy-done.3), custom_call_target="tpu_custom_call" | custom-call | tf_op jit(solution)/shard_map/pallas_call | solution.py:246
  55.4 17.5 %all_to_all.23.kick_ref = bf16[64,8,128]{2,1,0:T(8,128)(2,1)S(1)} all-to-all(bf16[64,8,128]{2,1,0:T(8,128)(2,1)S(1)} %shard_map.68), channel_id=1, replica_groups=mesh['bunch'=8,'zq'=4,'z0'=2,'y'=8] {'zq','z0','y'}, dimensions={0} | all-to-all | bytes 262144 | tf_op jit(solution)/shard_map/all_to_all | solution.py:200
  72.9 1.1 %shard_map.69 = bf16[64,2,512]{2,1,0:T(2,128)(2,1)} custom-call(bf16[64,8,128]{2,1,0:T(8,128)(2,1)S(1)} %all_to_all.23.kick_ref, s32[64,512]{1,0:T(8,128)S(1)} %copy-done), custom_call_target="tpu_custom_call" | custom-call | tf_op jit(solution)/shard_map/pallas_call | solution.py:253
  (3 shorter events, 0.1 us)
Async XLA Ops:
  0.0 1.3 %copy-start = (s32[64,512]{1,0:T(8,128)S(1)}, s32[64,512]{1,0:T(8,128)}, u32[]{:S(2)}) copy-start(s32[64,512]{1,0:T(8,128)} %index_ref.3) | copy-start | bytes 393220
  0.0 1.3 %copy-start.1 = (bf16[64,2,512]{2,1,0:T(2,128)(2,1)S(1)}, bf16[64,2,512]{2,1,0:T(2,128)(2,1)}, u32[]{:S(2)}) copy-start(bf16[64,2,512]{2,1,0:T(2,128)(2,1)} %coords_hbm.1) | copy-start | bytes 393220
  1.3 53.1 %copy-start.2 = (bf16[2,4,8,512]{3,2,1,0:T(8,128)(2,1)S(1)}, bf16[2,4,8,512]{3,2,1,0:T(8,128)(2,1)}, u32[]{:S(2)}) copy-start(bf16[2,4,8,512]{3,2,1,0:T(8,128)(2,1)} %panels_ref.1) | copy-start | bytes 196612
  1.3 53.1 %copy-start.3 = (s32[512]{0:T(512)S(1)}, s32[512]{0:T(512)}, u32[]{:S(2)}) copy-start(s32[512]{0:T(512)} %fill_ref.1) | copy-start | bytes 6148
  1.3 3.3 %collective-permute-start = (bf16[8,8,128]{2,1,0:T(8,128)(2,1)S(1)}, bf16[8,8,128]{2,1,0:T(8,128)(2,1)S(1)}, u32[]{:S(2)}, u32[]{:S(2)}) collective-permute-start(bf16[8,8,128]{2,1,0:T(8,128)(2,1)S(1)} %shard_map.65), channel_id=1, source_target_pairs={{0,64},{64,128},{128,192},{192,256},{256,320},{320,384},{384,448},... | collective-permute-start | bytes 49160 | tf_op jit(solution)/shard_map/ppermute | solution.py:228

commit v6 on v5

--- a/solution.py
+++ b/solution.py
@@ -19,23 +19,43 @@
 PARAMS = pltpu.CompilerParams(vmem_limit_bytes=32 * 1024 * 1024)
 
 
-def lane_ids(count):
-    return lax.broadcasted_iota(jnp.int32, (LANES, count), 0).astype(F32).astype(BF16)
-
-
-def bunch_moment(coords_ref, index_ref, b, ids):
+def patterns(count):
+    row = lax.broadcasted_iota(jnp.int32, (32, count), 0)
+    ids = row.astype(F32).astype(BF16)
+    tops = ((row & 3) * 4 + (row >> 3)).astype(F32).astype(BF16)
+    return ids, tops, (row & 4) == 0
+
+
+def four_moments(scale, coords_ref, index_ref, first, consts, rows, start):
     count = index_ref.shape[1]
-    row = index_ref[pl.ds(b, 1), :]
-    low = jnp.broadcast_to((row & (LANES - 1)).astype(F32).astype(BF16), (LANES, count))
-    onehot = jnp.where(low == ids, jnp.ones((), BF16), jnp.zeros((), BF16))
-    high = jnp.broadcast_to(row >> 7, (8, count))
-    planes = coords_ref[b].astype(F32)
-    sub = lax.broadcasted_iota(jnp.int32, (8, count), 0)
-    both = jnp.where(sub < 4, planes[0:1], planes[1:2])
-    left = jnp.where(high == (sub & 3), both, 0.0).astype(BF16)
-    return lax.dot_general(
-        left, onehot, (((1,), (1,)), ((), ())), preferred_element_type=F32
+    ids, tops, lower = consts
+    one, none = jnp.ones((), BF16), jnp.zeros((), BF16)
+    lefts, rights = [], []
+    for b in range(4):
+        index = index_ref[pl.ds(first + b, 1), :]
+        low = jnp.broadcast_to((index & 31).astype(F32).astype(BF16), (32, count))
+        top = jnp.broadcast_to((index >> 5).astype(F32).astype(BF16), (32, count))
+        planes = coords_ref[first + b].astype(F32)
+        near = jnp.broadcast_to(planes[0:1], (32, count))
+        far = jnp.broadcast_to(planes[1:2], (32, count))
+        both = jnp.where(lower, near, far).astype(BF16)
+        rights.append(jnp.where(low == ids, one, none))
+        lefts.append(jnp.where(top == tops, both, none))
+    product = lax.dot_general(
+        jnp.concatenate(lefts, 0),
+        jnp.concatenate(rights, 0),
+        (((1,), (1,)), ((), ())),
+        preferred_element_type=F32,
     )
+    block = lax.broadcasted_iota(jnp.int32, (8, LANES), 1) >> 5
+    for b in range(4):
+        total = None
+        for j in range(4):
+            part = product[b * 32 + j * 8 : b * 32 + j * 8 + 8]
+            if j != b:
+                part = pltpu.roll(part, 32 * ((j - b) % 4), 1)
+            total = part if total is None else jnp.where(block == j, part, total)
+        rows[pl.ds(pl.multiple_of(start + 8 * b, 8), 8), :] = scale * total
 
 
 def add_past_turns(hist, coef_ref, rows, first):
@@ -68,9 +88,9 @@
     copy_coef.start()
     copy_index.wait()
     copy_coords.wait()
-    ids = lane_ids(index.shape[1])
-    for b in range(8):
-        rows[pl.ds(8 * b, 8), :] = scale * bunch_moment(coords, index, b, ids)
+    consts = patterns(index.shape[1])
+    for first in (0, 4):
+        four_moments(scale, coords, index, first, consts, rows, 8 * first)
     copy_hist.wait()
     copy_coef.wait()
 
@@ -89,13 +109,13 @@
     copy_coef = pltpu.make_async_copy(coef_hbm, coef_ref, sems.at[1])
     copy_hist.start()
     copy_coef.start()
-    ids = lane_ids(index_ref.shape[1])
-
-    def one(b, _):
-        rows[pl.ds(pl.multiple_of(8 * b, 8), 8), :] = scale * bunch_moment(coords_ref, index_ref, b, ids)
+    consts = patterns(index_ref.shape[1])
+
+    def some(group, _):
+        four_moments(scale, coords_ref, index_ref, 4 * group, consts, rows, 32 * group)
         return 0
 
-    lax.fori_loop(0, bunches, one, 0, unroll=8)
+    lax.fori_loop(0, bunches // 4, some, 0, unroll=4)
     copy_hist.wait()
     copy_coef.wait()
     add_past_turns(hist, coef_ref, rows, dom * 8)

time: 74.3 us -> 72.9 us (0.981)
  Pallas kernels: 6.71 us -> 5.24 us
  waiting for transfers between devices: 0.01 us -> 1.23 us
  blocking collectives: 67.2 us -> 66 us
    pallas_call x1, Pallas kernels: 3.29 us -> 1.89 us  [local(): call(functools.partial(moment_kernel, scale), shape((16, 48, LANES), BF16...]
    ppermute x1, waiting for transfers between devices: 0.01 us -> 1.23 us  [local(): lax.ppermute(halo, 'bunch', [(i, (i + 1) % ring) for i in range(ring)])]
    all_to_all x4, blocking collectives: 67.2 us -> 66 us  [exchange(): return lax.all_to_all(value, axes, 0, 0, tiled=True)]
  transfers between devices with their start and end apart: 1 -> 1, of which waited for: 0 -> 1; matrix products, arithmetic and copies ran while one was open for 0% -> 0% of each run, Pallas kernels for 4% -> 3%
where the time goes in v6:
time: 72.9 us; the launch traced here: 72.6 us
  blocking collectives  66 us (91%)
  Pallas kernels  5.24 us (7%)
  waiting for transfers between devices  1.23 us (2%)
    all_to_all x4, blocking collectives, exchange(): return lax.all_to_all(value, axes, 0, 0, tiled=True)  66 us
    pallas_call x1, Pallas kernels, local(): call(functools.partial(moment_kernel, scale), shape((16, 48, LANES), BF16...  1.89 us
  transfers between devices with their start and end apart: 1, of which 1 were waited for; matrix products, arithmetic and copies ran while one was open for 0% of the time, Pallas kernels for 3%

profile of v6, /device:TPU:2, one launch (start us, length us, event | category | flops | bytes accessed | tf_op | source)
XLA Modules:
  0.0 72.6 jit_solution(12891605464832209735)
XLA Ops:
  0.0 0.0 copy-start
  0.0 0.0 copy-start.1
  0.0 1.2 %shard_map.65 = bf16[8,8,128]{2,1,0:T(8,128)(2,1)S(1)} custom-call(bf16[64,2,512]{2,1,0:T(2,128)(2,1)} %coords_hbm.1, s32[64,512]{1,0:T(8,128)} %index_ref.3, f32[64,16,2,512]{3,2,1,0:T(2,128)} %hist_hbm.3, f32[2,16]{1,0:T(2,128)} %bitcast.9), custom_call_target="tpu_custom_call" | custom-call | tf_op jit(solution)/shard_map/pallas_call | solution.py:234
  1.2 0.0 copy-start.2
  1.2 0.0 copy-start.3
  1.2 0.0 collective-permute-start
  1.2 0.0 copy-done
  1.2 0.0 copy-done.1
  1.3 1.9 %shard_map.64 = bf16[16,48,128]{2,1,0:T(8,128)(2,1)S(1)} custom-call(bf16[64,2,512]{2,1,0:T(2,128)(2,1)S(1)} %copy-done.1, s32[64,512]{1,0:T(8,128)S(1)} %copy-done, f32[64,16,2,512]{3,2,1,0:T(2,128)} %hist_hbm.3, f32[2,16]{1,0:T(2,128)} %bitcast.10), custom_call_target="tpu_custom_call" | custom-call | tf_op jit(solution)/shard_map/pallas_call | solution.py:249
  3.2 1.2 %collective-permute-done = bf16[8,8,128]{2,1,0:T(8,128)(2,1)S(1)} collective-permute-done((bf16[8,8,128]{2,1,0:T(8,128)(2,1)S(1)}, bf16[8,8,128]{2,1,0:T(8,128)(2,1)S(1)}, u32[]{:S(2)}, u32[]{:S(2)}) %collective-permute-start) | collective-permute-done | bytes 16416 | tf_op jit(solution)/shard_map/ppermute | solution.py:248
  4.4 18.1 %all_to_all.20.in_ref = bf16[16,48,128]{2,1,0:T(8,128)(2,1)S(1)} all-to-all(bf16[16,48,128]{2,1,0:T(8,128)(2,1)S(1)} %bitcast.8), channel_id=1, replica_groups=mesh['bunch'=8,'zq'=4,'z0'=2,'y'=8] {'z0','y'}, dimensions={0} | all-to-all | bytes 393216 | tf_op jit(solution)/shard_map/all_to_all | solution.py:220
  22.5 17.7 %all_to_all.21.in_ref = f32[4,40,128]{2,1,0:T(8,128)S(1)} all-to-all(f32[4,40,128]{2,1,0:T(8,128)S(1)} %shard_map.66), channel_id=1, replica_groups=mesh['bunch'=8,'zq'=4,'z0'=2,'y'=8] {'zq'}, dimensions={0} | all-to-all | bytes 163840 | tf_op jit(solution)/shard_map/all_to_all | solution.py:220
  40.2 13.0 %all_to_all.22.in_ref = bf16[16,48,128]{2,1,0:T(8,128)(2,1)S(1)} all-to-all(bf16[16,48,128]{2,1,0:T(8,128)(2,1)S(1)} %shard_map.67), channel_id=1, replica_groups=mesh['bunch'=8,'zq'=4,'z0'=2,'y'=8] {'z0','y'}, dimensions={0} | all-to-all | bytes 393216 | tf_op jit(solution)/shard_map/all_to_all | solution.py:220
  53.2 0.0 copy-done.2
  53.2 0.0 copy-done.3
  53.2 1.0 %shard_map.68 = bf16[64,8,128]{2,1,0:T(8,128)(2,1)S(1)} custom-call(bf16[16,48,128]{2,1,0:T(8,128)(2,1)S(1)} %all_to_all.22.in_ref, bf16[2,4,8,512]{3,2,1,0:T(8,128)(2,1)S(1)} %copy-done.2, s32[512]{0:T(512)S(1)} %copy-done.3), custom_call_target="tpu_custom_call" | custom-call | tf_op jit(solution)/shard_map/pallas_call | solution.py:266
  54.2 17.3 %all_to_all.23.kick_ref = bf16[64,8,128]{2,1,0:T(8,128)(2,1)S(1)} all-to-all(bf16[64,8,128]{2,1,0:T(8,128)(2,1)S(1)} %shard_map.68), channel_id=1, replica_groups=mesh['bunch'=8,'zq'=4,'z0'=2,'y'=8] {'zq','z0','y'}, dimensions={0} | all-to-all | bytes 262144 | tf_op jit(solution)/shard_map/all_to_all | solution.py:220
  71.5 1.1 %shard_map.69 = bf16[64,2,512]{2,1,0:T(2,128)(2,1)} custom-call(bf16[64,8,128]{2,1,0:T(8,128)(2,1)S(1)} %all_to_all.23.kick_ref, s32[64,512]{1,0:T(8,128)S(1)} %copy-done), custom_call_target="tpu_custom_call" | custom-call | tf_op jit(solution)/shard_map/pallas_call | solution.py:273
  (3 shorter events, 0.1 us)
Async XLA Ops:
  0.0 1.2 %copy-start = (s32[64,512]{1,0:T(8,128)S(1)}, s32[64,512]{1,0:T(8,128)}, u32[]{:S(2)}) copy-start(s32[64,512]{1,0:T(8,128)} %index_ref.3) | copy-start | bytes 393220
  0.0 1.2 %copy-start.1 = (bf16[64,2,512]{2,1,0:T(2,128)(2,1)S(1)}, bf16[64,2,512]{2,1,0:T(2,128)(2,1)}, u32[]{:S(2)}) copy-start(bf16[64,2,512]{2,1,0:T(2,128)(2,1)} %coords_hbm.1) | copy-start | bytes 393220
  1.2 52.0 %copy-start.2 = (bf16[2,4,8,512]{3,2,1,0:T(8,128)(2,1)S(1)}, bf16[2,4,8,512]{3,2,1,0:T(8,128)(2,1)}, u32[]{:S(2)}) copy-start(bf16[2,4,8,512]{3,2,1,0:T(8,128)(2,1)} %panels_ref.1) | copy-start | bytes 196612
  1.2 52.0 %copy-start.3 = (s32[512]{0:T(512)S(1)}, s32[512]{0:T(512)}, u32[]{:S(2)}) copy-start(s32[512]{0:T(512)} %fill_ref.1) | copy-start | bytes 6148
  1.2 3.2 %collective-permute-start = (bf16[8,8,128]{2,1,0:T(8,128)(2,1)S(1)}, bf16[8,8,128]{2,1,0:T(8,128)(2,1)S(1)}, u32[]{:S(2)}, u32[]{:S(2)}) collective-permute-start(bf16[8,8,128]{2,1,0:T(8,128)(2,1)S(1)} %shard_map.65), channel_id=1, source_target_pairs={{0,64},{64,128},{128,192},{192,256},{256,320},{320,384},{384,448},... | collective-permute-start | bytes 49160 | tf_op jit(solution)/shard_map/ppermute | solution.py:248

commit v7 on v6

--- a/solution.py
+++ b/solution.py
@@ -14,6 +14,7 @@
 DOM = ("zq", "z0", "y")
 ROW16 = ("z0", "y")
 COL4 = ("zq",)
+ROW8 = ("y",)
 VMEM = pl.BlockSpec(memory_space=pltpu.VMEM)
 HBM = pl.BlockSpec(memory_space=pltpu.HBM)
 PARAMS = pltpu.CompilerParams(vmem_limit_bytes=32 * 1024 * 1024)
@@ -143,7 +144,8 @@
         out_ref[copy] = total
 
 
-def kick_kernel(total_bunches, in_ref, panels_ref, fill_ref, out_ref, source, bucket):
+def kick_kernel(total_bunches, in_ref, mine_ref, got_ref, fill_ref, out_ref, source, bucket):
+    plane = lax.axis_index("z0")
     bunches = 64
     first = lax.axis_index("bunch") * bunches
     sub = lax.broadcasted_iota(jnp.int32, (8, LANES), 0)
@@ -154,41 +156,46 @@
             place = jnp.where(place >= total_bunches, place - total_bunches, place)
             column = jnp.where(sub == row, fill_ref[place], column)
         bucket[pl.ds(tile * 8, 8), :] = column
-    for ph in range(8):
-        source[ph, pl.ds(0, 40), :] = in_ref[2 * ph].astype(F32)[0:40]
-        source[ph, pl.ds(40, 32), :] = in_ref[2 * ph + 1].astype(F32)[8:40]
+    for high in range(4):
+        source[high, pl.ds(0, 40), :] = in_ref[2 * high].astype(F32)[0:40]
+        source[high, pl.ds(40, 32), :] = in_ref[2 * high + 1].astype(F32)[8:40]
     cycle = 2 * total_bunches
     here = bucket[pl.ds(8, bunches), :]
     gaps = [None] + [(here - bucket[pl.ds(8 - d, bunches), :]) & (cycle - 1) for d in (1, 2, 3)]
+    picked = [[], [], [], []]
+    for high in range(4):
+        past = [source[high, pl.ds(8 - d, bunches), :] for d in range(4)]
+        picked[0].append(past[0].astype(BF16))
+        for k in (1, 2, 3):
+            value = jnp.zeros((bunches, LANES), F32)
+            for d in range(1, k + 1):
+                value = jnp.where(gaps[d] == k, past[d], value)
+            picked[k].append(value.astype(BF16))
     outs = []
-    for plane in range(2):
-        picked = [[], [], [], []]
-        for high in range(4):
-            ph = plane * 4 + high
-            past = [source[ph, pl.ds(8 - d, bunches), :] for d in range(4)]
-            picked[0].append(past[0].astype(BF16))
-            for k in (1, 2, 3):
-                value = jnp.zeros((bunches, LANES), F32)
-                for d in range(1, k + 1):
-                    value = jnp.where(gaps[d] == k, past[d], value)
-                picked[k].append(value.astype(BF16))
+    for panels_ref in (mine_ref, got_ref):
         total = None
         for k in range(4):
             right = jnp.concatenate(picked[k], 1)
-            left = panels_ref[plane, k]
-            part = lax.dot_general(left, right, (((1,), (1,)), ((), ())), preferred_element_type=F32)
+            part = lax.dot_general(
+                panels_ref[plane, k], right, (((1,), (1,)), ((), ())), preferred_element_type=F32
+            )
             total = part if total is None else total + part
         outs.append(total)
-    kick = jnp.concatenate(outs, 1).astype(BF16)
+    kick = jnp.where(plane == 0, jnp.concatenate(outs, 1), jnp.concatenate(outs[::-1], 1)).astype(BF16)
     for copy in range(out_ref.shape[0]):
         out_ref[copy] = kick
 
 
 def lookup_kernel(kick_ref, index_ref, out_ref, table):
     bunches = index_ref.shape[0]
+    half = LANES // 2
+    lower = lax.broadcasted_iota(jnp.int32, (half, LANES), 1) < half
     for high in range(4):
         rows = jnp.concatenate([kick_ref[16 * high + part].astype(F32) for part in range(16)], 0)
-        table[high] = rows.T
+        turned = rows.T
+        first, second = turned[0:half], turned[half:]
+        table[high, pl.ds(0, half), :] = jnp.where(lower, first, pltpu.roll(second, half, 1))
+        table[high, pl.ds(half, half), :] = jnp.where(lower, pltpu.roll(first, half, 1), second)
     for block in range(bunches // 8):
         for tile in range(index_ref.shape[1] // LANES):
             index = index_ref[pl.ds(block * 8, 8), pl.ds(tile * LANES, LANES)]
@@ -246,6 +253,7 @@
     )(far(coords, pltpu.HBM), far(slice_index, pltpu.HBM), past, coef)
     ring = lax.axis_size("bunch")
     halo = lax.ppermute(halo, "bunch", [(i, (i + 1) % ring) for i in range(ring)])
+    got = lax.ppermute(panels, "z0", [(0, 1), (1, 0)])
     partial = call(
         functools.partial(moment_kernel, scale),
         shape((16, 48, LANES), BF16),
@@ -259,16 +267,17 @@
     )(coords, slice_index, past, coef)
     partial = partial.reshape(8, 2, 48, LANES).at[:, 0, 0:8].set(halo).reshape(16, 48, LANES)
     part = exchange(partial, ROW16)
+    part, got = lax.optimization_barrier((part, got))
     part = call(sum_kernel, shape((4, 40, LANES), F32), [VMEM])(part)
     part = exchange(part, COL4)
-    source = call(source_kernel, shape((16, 48, LANES), BF16), [VMEM])(part)
-    source = exchange(source, ROW16)
+    source = call(source_kernel, shape((8, 48, LANES), BF16), [VMEM])(part)
+    source = exchange(source, ROW8)
     kick = call(
         functools.partial(kick_kernel, bunches * ring),
         shape((64, 8, LANES), BF16),
-        [VMEM, VMEM, smem],
-        [pltpu.VMEM((8, 72, LANES), F32), pltpu.VMEM((72, LANES), jnp.int32)],
-    )(source, panels, fill)
+        [VMEM, VMEM, VMEM, smem],
+        [pltpu.VMEM((4, 72, LANES), F32), pltpu.VMEM((72, LANES), jnp.int32)],
+    )(source, panels, got, fill)
     kick = exchange(kick, DOM)
     return call(
         lookup_kernel,

time: 72.9 us -> 73.7 us (1.011)
  blocking collectives: 66 us -> 47.2 us
  starting transfers between devices: 0.02 us -> 12.9 us
  waiting for transfers between devices: 1.23 us -> 6.62 us
  Pallas kernels: 5.24 us -> 6 us
    all_to_all x4 -> x3, blocking collectives: 66 us -> 47.2 us  [exchange(): return lax.all_to_all(value, axes, 0, 0, tiled=True)]
    all_to_all x0 -> x1, starting transfers between devices: none -> 9.02 us  [exchange(): return lax.all_to_all(value, axes, 0, 0, tiled=True)]
    ppermute x0 -> x1, starting transfers between devices: none -> 3.83 us  [local(): got = lax.ppermute(panels, 'z0', [(0, 1), (1, 0)])]
    ppermute x0 -> x1, waiting for transfers between devices: none -> 3.58 us  [local(): got = lax.ppermute(panels, 'z0', [(0, 1), (1, 0)])]
    all_to_all x0 -> x1, waiting for transfers between devices: none -> 2.49 us  [exchange(): return lax.all_to_all(value, axes, 0, 0, tiled=True)]
  transfers between devices with their start and end apart: 1 -> 3, of which waited for: 1 -> 3; matrix products, arithmetic and copies ran while one was open for 0% -> 0% of each run, Pallas kernels for 3% -> 3%
where the time goes in v7:
time: 73.7 us; the launch traced here: 73.4 us
  blocking collectives  47.2 us (64%)
  starting transfers between devices  12.9 us (18%)
  waiting for transfers between devices  6.62 us (9%)
  Pallas kernels  6 us (8%)
    all_to_all x3, blocking collectives, exchange(): return lax.all_to_all(value, axes, 0, 0, tiled=True)  47.2 us
    all_to_all x1, starting transfers between devices, exchange(): return lax.all_to_all(value, axes, 0, 0, tiled=True)  9.02 us
    ppermute x1, starting transfers between devices, local(): got = lax.ppermute(panels, 'z0', [(0, 1), (1, 0)])  3.83 us
    ppermute x1, waiting for transfers between devices, local(): got = lax.ppermute(panels, 'z0', [(0, 1), (1, 0)])  3.58 us
    pallas_call x1, Pallas kernels, local(): call(functools.partial(moment_kernel, scale), shape((16, 48, LANES), BF16...  2.56 us
    all_to_all x1, waiting for transfers between devices, exchange(): return lax.all_to_all(value, axes, 0, 0, tiled=True)  2.49 us
  transfers between devices with their start and end apart: 3, of which 3 were waited for; matrix products, arithmetic and copies ran while one was open for 0% of the time, Pallas kernels for 3%

profile of v7, /device:TPU:2, one launch (start us, length us, event | category | flops | bytes accessed | tf_op | source)
XLA Modules:
  0.0 73.4 jit_solution(491145876433211477)
XLA Ops:
  0.0 0.0 copy-start.1
  0.0 0.0 copy-start
  0.0 0.0 copy-start.2
  0.0 0.0 copy-start.3
  0.0 1.2 %shard_map.65 = bf16[8,8,128]{2,1,0:T(8,128)(2,1)S(1)} custom-call(bf16[64,2,512]{2,1,0:T(2,128)(2,1)} %coords_hbm.1, s32[64,512]{1,0:T(8,128)} %index_ref.3, f32[64,16,2,512]{3,2,1,0:T(2,128)} %hist_hbm.3, f32[2,16]{1,0:T(2,128)} %bitcast.7), custom_call_target="tpu_custom_call" | custom-call | tf_op jit(solution)/shard_map/pallas_call | solution.py:241
  1.2 0.0 collective-permute-start
  1.2 0.0 copy-done.1
  1.2 0.0 copy-done
  1.2 2.6 %shard_map.64 = bf16[16,48,128]{2,1,0:T(8,128)(2,1)} custom-call(bf16[64,2,512]{2,1,0:T(2,128)(2,1)S(1)} %copy-done.1, s32[64,512]{1,0:T(8,128)S(1)} %copy-done, f32[64,16,2,512]{3,2,1,0:T(2,128)} %hist_hbm.3, f32[2,16]{1,0:T(2,128)} %bitcast.8), custom_call_target="tpu_custom_call" | custom-call | tf_op jit(solution)/shard_map/pallas_call | solution.py:257
  3.8 0.6 collective-permute-done
  4.4 0.6 bitcast_dynamic-update-slice_fusion
  5.0 9.0 %all-to-all-start = ((bf16[16,48,128]{2,1,0:T(8,128)(2,1)}), bf16[16,48,128]{2,1,0:T(8,128)(2,1)S(1)}, u32[]{:S(2)}, u32[]{:S(2)}) async-start(bf16[16,48,128]{2,1,0:T(8,128)(2,1)} %bitcast.4), calls=%async_computation | async-start | bytes 393216 | tf_op jit(solution)/shard_map/all_to_all | solution.py:227
  14.0 0.0 copy-done.2
  14.0 3.8 %collective-permute-start.1 = (bf16[2,4,8,512]{3,2,1,0:T(8,128)(2,1)S(1)}, bf16[2,4,8,512]{3,2,1,0:T(8,128)(2,1)S(1)}, u32[]{:S(2)}, u32[]{:S(2)}) collective-permute-start(bf16[2,4,8,512]{3,2,1,0:T(8,128)(2,1)S(1)} %copy-done.2), channel_id=1, source_target_pairs={{0,8},{8,0},{1,9},{9,1},{2,10},{10,2},{3,11},{11,3},{4,12},{12,4},... | collective-permute-start | bytes 196616 | tf_op jit(solution)/shard_map/ppermute | solution.py:256
  17.8 3.6 %collective-permute-done.1.got_ref = bf16[2,4,8,512]{3,2,1,0:T(8,128)(2,1)S(1)} collective-permute-done((bf16[2,4,8,512]{3,2,1,0:T(8,128)(2,1)S(1)}, bf16[2,4,8,512]{3,2,1,0:T(8,128)(2,1)S(1)}, u32[]{:S(2)}, u32[]{:S(2)}) %collective-permute-start.1) | collective-permute-done | bytes 65568 | tf_op jit(solution)/shard_map/ppermute | solution.py:256
  21.4 2.5 %all-to-all-done.in_ref = bf16[16,48,128]{2,1,0:T(8,128)(2,1)S(1)} async-done(((bf16[16,48,128]{2,1,0:T(8,128)(2,1)}), bf16[16,48,128]{2,1,0:T(8,128)(2,1)S(1)}, u32[]{:S(2)}, u32[]{:S(2)}) %all-to-all-start) | async-done | bytes 196640 | tf_op jit(solution)/shard_map/all_to_all | solution.py:227
  23.9 17.7 %all_to_all.20.in_ref = f32[4,40,128]{2,1,0:T(8,128)S(1)} all-to-all(f32[4,40,128]{2,1,0:T(8,128)S(1)} %shard_map.66), channel_id=1, replica_groups=mesh['bunch'=8,'zq'=4,'z0'=2,'y'=8] {'zq'}, dimensions={0} | all-to-all | bytes 163840 | tf_op jit(solution)/shard_map/all_to_all | solution.py:227
  41.6 13.0 %all_to_all.21.in_ref = bf16[8,48,128]{2,1,0:T(8,128)(2,1)S(1)} all-to-all(bf16[8,48,128]{2,1,0:T(8,128)(2,1)S(1)} %shard_map.67), channel_id=1, replica_groups=mesh['bunch'=8,'zq'=4,'z0'=2,'y'=8] {'y'}, dimensions={0} | all-to-all | bytes 196608 | tf_op jit(solution)/shard_map/all_to_all | solution.py:227
  54.6 0.0 copy-done.3
  54.6 1.0 %shard_map.68 = bf16[64,8,128]{2,1,0:T(8,128)(2,1)S(1)} custom-call(bf16[8,48,128]{2,1,0:T(8,128)(2,1)S(1)} %all_to_all.21.in_ref, bf16[2,4,8,512]{3,2,1,0:T(8,128)(2,1)S(1)} %copy-done.2, bf16[2,4,8,512]{3,2,1,0:T(8,128)(2,1)S(1)} %collective-permute-done.1.got_ref, s32[512]{0:T(512)S(1)} %copy-done.3), custom_call_target="tpu_custom_call" | custom-call | tf_op jit(solution)/shard_map/pallas_call | solution.py:275
  55.7 16.5 %all_to_all.22.kick_ref = bf16[64,8,128]{2,1,0:T(8,128)(2,1)S(1)} all-to-all(bf16[64,8,128]{2,1,0:T(8,128)(2,1)S(1)} %shard_map.68), channel_id=1, replica_groups=mesh['bunch'=8,'zq'=4,'z0'=2,'y'=8] {'zq','z0','y'}, dimensions={0} | all-to-all | bytes 262144 | tf_op jit(solution)/shard_map/all_to_all | solution.py:227
  72.1 1.2 %shard_map.69 = bf16[64,2,512]{2,1,0:T(2,128)(2,1)} custom-call(bf16[64,8,128]{2,1,0:T(8,128)(2,1)S(1)} %all_to_all.22.kick_ref, s32[64,512]{1,0:T(8,128)S(1)} %copy-done), custom_call_target="tpu_custom_call" | custom-call | tf_op jit(solution)/shard_map/pallas_call | solution.py:282
  (2 shorter events, 0.0 us)
Async XLA Ops:
  0.0 1.2 %copy-start.1 = (bf16[64,2,512]{2,1,0:T(2,128)(2,1)S(1)}, bf16[64,2,512]{2,1,0:T(2,128)(2,1)}, u32[]{:S(2)}) copy-start(bf16[64,2,512]{2,1,0:T(2,128)(2,1)} %coords_hbm.1) | copy-start | bytes 393220
  0.0 1.2 %copy-start = (s32[64,512]{1,0:T(8,128)S(1)}, s32[64,512]{1,0:T(8,128)}, u32[]{:S(2)}) copy-start(s32[64,512]{1,0:T(8,128)} %index_ref.3) | copy-start | bytes 393220
  0.0 14.0 %copy-start.2 = (bf16[2,4,8,512]{3,2,1,0:T(8,128)(2,1)S(1)}, bf16[2,4,8,512]{3,2,1,0:T(8,128)(2,1)}, u32[]{:S(2)}) copy-start(bf16[2,4,8,512]{3,2,1,0:T(8,128)(2,1)} %mine_ref.1) | copy-start | bytes 196612
  0.0 54.6 %copy-start.3 = (s32[512]{0:T(512)S(1)}, s32[512]{0:T(512)}, u32[]{:S(2)}) copy-start(s32[512]{0:T(512)} %fill_ref.1) | copy-start | bytes 6148
  1.2 3.2 %collective-permute-start = (bf16[8,8,128]{2,1,0:T(8,128)(2,1)S(1)}, bf16[8,8,128]{2,1,0:T(8,128)(2,1)S(1)}, u32[]{:S(2)}, u32[]{:S(2)}) collective-permute-start(bf16[8,8,128]{2,1,0:T(8,128)(2,1)S(1)} %shard_map.65), channel_id=1, source_target_pairs={{0,64},{64,128},{128,192},{192,256},{256,320},{320,384},{384,448},... | collective-permute-start | bytes 49160 | tf_op jit(solution)/shard_map/ppermute | solution.py:255
  5.0 18.9 %all-to-all-start = ((bf16[16,48,128]{2,1,0:T(8,128)(2,1)}), bf16[16,48,128]{2,1,0:T(8,128)(2,1)S(1)}, u32[]{:S(2)}, u32[]{:S(2)}) async-start(bf16[16,48,128]{2,1,0:T(8,128)(2,1)} %bitcast.4), calls=%async_computation | async-start | bytes 393216 | tf_op jit(solution)/shard_map/all_to_all | solution.py:227
  14.0 7.4 %collective-permute-start.1 = (bf16[2,4,8,512]{3,2,1,0:T(8,128)(2,1)S(1)}, bf16[2,4,8,512]{3,2,1,0:T(8,128)(2,1)S(1)}, u32[]{:S(2)}, u32[]{:S(2)}) collective-permute-start(bf16[2,4,8,512]{3,2,1,0:T(8,128)(2,1)S(1)} %copy-done.2), channel_id=1, source_target_pairs={{0,8},{8,0},{1,9},{9,1},{2,10},{10,2},{3,11},{11,3},{4,12},{12,4},... | collective-permute-start | bytes 196616 | tf_op jit(solution)/shard_map/ppermute | solution.py:256

commit v8 on v6

--- a/solution.py
+++ b/solution.py
@@ -11,9 +11,9 @@
 F32 = jnp.float32
 BF16 = jnp.bfloat16
 LANES = 128
-DOM = ("zq", "z0", "y")
-ROW16 = ("z0", "y")
-COL4 = ("zq",)
+DOM = ("z", "yq", "y0")
+ROW16 = ("z", "y0")
+COL4 = ("yq",)
 VMEM = pl.BlockSpec(memory_space=pltpu.VMEM)
 HBM = pl.BlockSpec(memory_space=pltpu.HBM)
 PARAMS = pltpu.CompilerParams(vmem_limit_bytes=32 * 1024 * 1024)
@@ -279,7 +279,7 @@
 
 
 def solution(mesh):
-    fine = Mesh(mesh.devices.reshape(8, 4, 2, 8), ("bunch", "zq", "z0", "y"))
+    fine = Mesh(mesh.devices.reshape(8, 8, 4, 2), ("bunch", "z", "yq", "y0"))
     return jax.shard_map(
         local,
         mesh=fine,

time: 72.9 us -> 72 us (0.988)
  blocking collectives: 66 us -> 65.2 us
    all_to_all x4, blocking collectives: 66 us -> 65.2 us  [exchange(): return lax.all_to_all(value, axes, 0, 0, tiled=True)]
where the time goes in v8:
time: 72 us; the launch traced here: 71.8 us
  blocking collectives  65.2 us (91%)
  Pallas kernels  5.24 us (7%)
  waiting for transfers between devices  1.23 us (2%)
    all_to_all x4, blocking collectives, exchange(): return lax.all_to_all(value, axes, 0, 0, tiled=True)  65.2 us
    pallas_call x1, Pallas kernels, local(): call(functools.partial(moment_kernel, scale), shape((16, 48, LANES), BF16...  1.89 us
  transfers between devices with their start and end apart: 1, of which 1 were waited for; matrix products, arithmetic and copies ran while one was open for 0% of the time, Pallas kernels for 3%

profile of v8, /device:TPU:2, one launch (start us, length us, event | category | flops | bytes accessed | tf_op | source)
XLA Modules:
  0.0 71.8 jit_solution(12077835208632418270)
XLA Ops:
  0.0 0.0 copy-start
  0.0 0.0 copy-start.1
  0.0 1.2 %shard_map.65 = bf16[8,8,128]{2,1,0:T(8,128)(2,1)S(1)} custom-call(bf16[64,2,512]{2,1,0:T(2,128)(2,1)} %coords_hbm.1, s32[64,512]{1,0:T(8,128)} %index_ref.3, f32[64,16,2,512]{3,2,1,0:T(2,128)} %hist_hbm.3, f32[2,16]{1,0:T(2,128)} %bitcast.9), custom_call_target="tpu_custom_call" | custom-call | tf_op jit(solution)/shard_map/pallas_call | solution.py:234
  1.2 0.0 copy-start.2
  1.2 0.0 copy-start.3
  1.2 0.0 collective-permute-start
  1.2 0.0 copy-done
  1.2 0.0 copy-done.1
  1.3 1.9 %shard_map.64 = bf16[16,48,128]{2,1,0:T(8,128)(2,1)S(1)} custom-call(bf16[64,2,512]{2,1,0:T(2,128)(2,1)S(1)} %copy-done.1, s32[64,512]{1,0:T(8,128)S(1)} %copy-done, f32[64,16,2,512]{3,2,1,0:T(2,128)} %hist_hbm.3, f32[2,16]{1,0:T(2,128)} %bitcast.10), custom_call_target="tpu_custom_call" | custom-call | tf_op jit(solution)/shard_map/pallas_call | solution.py:249
  3.2 1.2 %collective-permute-done = bf16[8,8,128]{2,1,0:T(8,128)(2,1)S(1)} collective-permute-done((bf16[8,8,128]{2,1,0:T(8,128)(2,1)S(1)}, bf16[8,8,128]{2,1,0:T(8,128)(2,1)S(1)}, u32[]{:S(2)}, u32[]{:S(2)}) %collective-permute-start) | collective-permute-done | bytes 16416 | tf_op jit(solution)/shard_map/ppermute | solution.py:248
  4.4 22.0 %all_to_all.20.in_ref = bf16[16,48,128]{2,1,0:T(8,128)(2,1)S(1)} all-to-all(bf16[16,48,128]{2,1,0:T(8,128)(2,1)S(1)} %bitcast.8), channel_id=1, replica_groups=mesh['bunch'=8,'z'=8,'yq'=4,'y0'=2] {'z','y0'}, dimensions={0} | all-to-all | bytes 393216 | tf_op jit(solution)/shard_map/all_to_all | solution.py:220
  26.5 14.4 %all_to_all.21.in_ref = f32[4,40,128]{2,1,0:T(8,128)S(1)} all-to-all(f32[4,40,128]{2,1,0:T(8,128)S(1)} %shard_map.66), channel_id=1, replica_groups=mesh['bunch'=8,'z'=8,'yq'=4,'y0'=2] {'yq'}, dimensions={0} | all-to-all | bytes 163840 | tf_op jit(solution)/shard_map/all_to_all | solution.py:220
  40.9 12.2 %all_to_all.22.in_ref = bf16[16,48,128]{2,1,0:T(8,128)(2,1)S(1)} all-to-all(bf16[16,48,128]{2,1,0:T(8,128)(2,1)S(1)} %shard_map.67), channel_id=1, replica_groups=mesh['bunch'=8,'z'=8,'yq'=4,'y0'=2] {'z','y0'}, dimensions={0} | all-to-all | bytes 393216 | tf_op jit(solution)/shard_map/all_to_all | solution.py:220
  53.1 0.0 copy-done.2
  53.1 0.0 copy-done.3
  53.1 1.0 %shard_map.68 = bf16[64,8,128]{2,1,0:T(8,128)(2,1)S(1)} custom-call(bf16[16,48,128]{2,1,0:T(8,128)(2,1)S(1)} %all_to_all.22.in_ref, bf16[2,4,8,512]{3,2,1,0:T(8,128)(2,1)S(1)} %copy-done.2, s32[512]{0:T(512)S(1)} %copy-done.3), custom_call_target="tpu_custom_call" | custom-call | tf_op jit(solution)/shard_map/pallas_call | solution.py:266
  54.2 16.5 %all_to_all.23.kick_ref = bf16[64,8,128]{2,1,0:T(8,128)(2,1)S(1)} all-to-all(bf16[64,8,128]{2,1,0:T(8,128)(2,1)S(1)} %shard_map.68), channel_id=1, replica_groups=mesh['bunch'=8,'z'=8,'yq'=4,'y0'=2] {'z','yq','y0'}, dimensions={0} | all-to-all | bytes 262144 | tf_op jit(solution)/shard_map/all_to_all | solution.py:220
  70.7 1.1 %shard_map.69 = bf16[64,2,512]{2,1,0:T(2,128)(2,1)} custom-call(bf16[64,8,128]{2,1,0:T(8,128)(2,1)S(1)} %all_to_all.23.kick_ref, s32[64,512]{1,0:T(8,128)S(1)} %copy-done), custom_call_target="tpu_custom_call" | custom-call | tf_op jit(solution)/shard_map/pallas_call | solution.py:273
  (3 shorter events, 0.1 us)
Async XLA Ops:
  0.0 1.2 %copy-start = (s32[64,512]{1,0:T(8,128)S(1)}, s32[64,512]{1,0:T(8,128)}, u32[]{:S(2)}) copy-start(s32[64,512]{1,0:T(8,128)} %index_ref.3) | copy-start | bytes 393220
  0.0 1.2 %copy-start.1 = (bf16[64,2,512]{2,1,0:T(2,128)(2,1)S(1)}, bf16[64,2,512]{2,1,0:T(2,128)(2,1)}, u32[]{:S(2)}) copy-start(bf16[64,2,512]{2,1,0:T(2,128)(2,1)} %coords_hbm.1) | copy-start | bytes 393220
  1.2 51.9 %copy-start.2 = (bf16[2,4,8,512]{3,2,1,0:T(8,128)(2,1)S(1)}, bf16[2,4,8,512]{3,2,1,0:T(8,128)(2,1)}, u32[]{:S(2)}) copy-start(bf16[2,4,8,512]{3,2,1,0:T(8,128)(2,1)} %panels_ref.1) | copy-start | bytes 196612
  1.2 51.9 %copy-start.3 = (s32[512]{0:T(512)S(1)}, s32[512]{0:T(512)}, u32[]{:S(2)}) copy-start(s32[512]{0:T(512)} %fill_ref.1) | copy-start | bytes 6148
  1.2 3.2 %collective-permute-start = (bf16[8,8,128]{2,1,0:T(8,128)(2,1)S(1)}, bf16[8,8,128]{2,1,0:T(8,128)(2,1)S(1)}, u32[]{:S(2)}, u32[]{:S(2)}) collective-permute-start(bf16[8,8,128]{2,1,0:T(8,128)(2,1)S(1)} %shard_map.65), channel_id=1, source_target_pairs={{0,64},{64,128},{128,192},{192,256},{256,320},{320,384},{384,448},... | collective-permute-start | bytes 49160 | tf_op jit(solution)/shard_map/ppermute | solution.py:248
